TPU v7x, 1024 devices: a whole 4x4x32 slice. The times are simulated.
1024 devices in a mesh: dp: 16 (over z_hi, y), expert: 64 (over z_lo, x, core).
Axes of the slice: x: 4, y: 4, z: 32 (z_hi: 4, z_lo: 8; z = z_hi * 8 + z_lo), core: 2. Of those that a mesh axis runs over, the one named last changes fastest.
Arguments:
- grad_out: bfloat16 [131072, 4096], P(('dp', 'expert')), may hold values from -2 to 2
- expert_ids: int32 [131072], P(('dp', 'expert')), may hold values from 0 to 63, as said below
- gate_weight: bfloat16 [131072], P(('dp', 'expert')), may hold values from 0.099609375 to 1
- saved_hidden: bfloat16 [16, 64, 192, 768], P('dp', 'expert'), may hold values from -6 to 6
- down_weight: bfloat16 [64, 768, 4096], P('expert'), may hold values from -0.21875 to 0.21875
- adapter_a: bfloat16 [64, 32, 768], P('expert'), may hold values from -0.21875 to 0.21875
- adapter_b: bfloat16 [64, 32, 4096], P('expert'), may hold values from -1 to 1
Outputs:
- hidden_gradient: bfloat16 [16, 64, 192, 768], P('dp', 'expert')
- gate_grad: float32 [131072], P(('dp', 'expert'))
- adapter_a_grad: float32 [64, 32, 768], P('expert')
- adapter_b_grad: float32 [64, 32, 4096], P('expert')
Inputs may be any that keep to these rules, and one draw needn't show every extreme that they name: `expert_ids`: in each block of 128 tokens that one device holds, no expert is named by more than 3 tokens, and one expert, drawn from the seed, is named by exactly 3 tokens in every block.
All inputs are finite; a program needn't handle non-finite values.
Results may differ from a plain program's by a relative error of at most 0.0049.
Values may be sent and summed in bfloat16 or wider, within the bound.
No kernel may reach another device: no remote copies, remote signals or barrier semaphores. Data moves between devices by JAX's collectives and lax.ppermute only.
A program may use at most 64 MiB of HBM per device.

v0:
```python
import jax
import jax.numpy as jnp
from jax import lax
from jax.sharding import PartitionSpec as P

adapter_scale = 2.0


def sum_adapters(grad_rows, gate_values, adapter_proj, reduced_rank_rows, hidden_activation_rows):
    gate_scaled_rows = (gate_values[:, None] * grad_rows.astype(jnp.float32)).astype(jnp.bfloat16)
    second_factor_gradient = adapter_scale * jnp.dot(
        reduced_rank_rows.T, gate_scaled_rows, preferred_element_type=jnp.float32
    )
    scaled_projection = (gate_values[:, None] * adapter_proj).astype(jnp.bfloat16)
    first_factor_gradient = adapter_scale * jnp.dot(
        scaled_projection.T, hidden_activation_rows, preferred_element_type=jnp.float32
    )
    return lax.psum((first_factor_gradient, second_factor_gradient), "dp")


def shards(grad_out, expert_ids, gate_weight, saved_hidden, down_weight, adapter_a, adapter_b):
    experts = lax.axis_size("expert")
    capacity = saved_hidden.shape[2] // experts
    labels = jnp.arange(experts, dtype=jnp.int32)
    onehot = (expert_ids[:, None] == labels[None, :]).astype(jnp.int32)
    token_rank = jnp.sum((jnp.cumsum(onehot, axis=0) - onehot) * onehot, axis=1)
    slot_index = expert_ids * capacity + token_rank
    chosen = (
        jnp.arange(experts * capacity, dtype=jnp.int32)[:, None] == slot_index[None, :]
    ).astype(jnp.bfloat16)
    outgoing = jnp.dot(chosen, grad_out, preferred_element_type=jnp.float32).astype(jnp.bfloat16)
    outgoing_gate = jnp.dot(chosen, gate_weight[:, None], preferred_element_type=jnp.float32)[
        :, 0
    ].astype(jnp.bfloat16)
    arrived, arrived_gate = (
        lax.all_to_all(
            outgoing.reshape(experts, capacity, -1),
            "expert",
            split_axis=0,
            concat_axis=0,
            tiled=True,
        ),
        lax.all_to_all(
            outgoing_gate.reshape(experts, capacity),
            "expert",
            split_axis=0,
            concat_axis=0,
            tiled=True,
        ),
    )
    grad_rows = arrived.reshape(experts * capacity, -1)
    gate_values = arrived_gate.reshape(-1).astype(jnp.float32)
    hidden_activation_rows = saved_hidden.reshape(experts * capacity, -1)
    weight = down_weight[0]
    factor_a = adapter_a[0]
    second_factor = adapter_b[0]
    reduced_rank_rows = jnp.dot(
        hidden_activation_rows, factor_a.T, preferred_element_type=jnp.float32
    ).astype(jnp.bfloat16)
    adapter_proj = lax.dot_general(
        grad_rows, second_factor, (((1,), (1,)), ((), ())), preferred_element_type=jnp.float32
    )
    projected_rows = lax.dot_general(
        grad_rows, weight, (((1,), (1,)), ((), ())), preferred_element_type=jnp.float32
    )
    rounded_proj = adapter_proj.astype(jnp.bfloat16)
    backward_product = jnp.dot(rounded_proj, factor_a, preferred_element_type=jnp.float32)
    hidden_gradient = (
        gate_values[:, None] * (projected_rows + adapter_scale * backward_product)
    ).astype(jnp.bfloat16)
    output_gradient_rows = jnp.dot(
        hidden_activation_rows, weight, preferred_element_type=jnp.float32
    )
    output_gradient_rows = output_gradient_rows + adapter_scale * jnp.dot(
        reduced_rank_rows, second_factor, preferred_element_type=jnp.float32
    )
    gate_terms = jnp.sum(grad_rows.astype(jnp.float32) * output_gradient_rows, axis=1)
    summed_a, summed_b = sum_adapters(
        grad_rows, gate_values, adapter_proj, reduced_rank_rows, hidden_activation_rows
    )
    came_back = lax.all_to_all(
        gate_terms.reshape(experts, capacity), "expert", split_axis=0, concat_axis=0, tiled=True
    )
    gate_grad = jnp.sum(jnp.where(chosen > 0, came_back.reshape(-1)[:, None], 0.0), axis=0)
    return (hidden_gradient.reshape(saved_hidden.shape), gate_grad, summed_a[None], summed_b[None])


def solution(mesh):
    in_specs = (
        P(("dp", "expert"), None),
        P(("dp", "expert")),
        P(("dp", "expert")),
        P("dp", "expert", None, None),
        P("expert", None, None),
        P("expert", None, None),
        P("expert", None, None),
    )
    out_specs = (
        P("dp", "expert", None, None),
        P(("dp", "expert")),
        P("expert", None, None),
        P("expert", None, None),
    )
    return jax.shard_map(shards, mesh=mesh, in_specs=in_specs, out_specs=out_specs, check_vma=False)
```

profile of v0, /device:TPU:6, one launch (start us, length us, event | category | flops | bytes accessed | tf_op | source)
XLA Modules:
  0.0 475.6 jit_solution(222792639986862561)
XLA Ops:
  7.2 0.0 copy-start
  7.2 0.8 fusion.24
  8.0 0.2 reduce_window_sum.11
  8.2 0.8 select_reduce_fusion.1
  9.0 0.7 multiply_add_fusion
  9.7 0.8 fusion.23
  10.5 0.8 convert_element_type.66
  11.3 17.2 %all-to-all-start = ((bf16[64,1,3]{2,1,0:T(2,128)(2,1)}), bf16[64,1,3]{2,1,0:T(2,128)(2,1)S(1)}, u32[]{:S(2)}, u32[]{:S(2)}) async-start(bf16[64,1,3]{2,1,0:T(2,128)(2,1)} %convert_element_type.66), calls=%async_computation | async-start | bytes 65536 | tf_op jit(solution)/shard_map/all_to_all | solution.py:43
  28.5 0.0 copy-done
  28.5 0.6 convolution_convert_fusion
  29.1 0.0 copy-start.1
  29.1 0.0 copy-start.3
  29.1 2.4 reshape.56
  31.5 7.8 %all-to-all-done = bf16[64,1,3]{2,1,0:T(2,128)(2,1)S(1)} async-done(((bf16[64,1,3]{2,1,0:T(2,128)(2,1)}), bf16[64,1,3]{2,1,0:T(2,128)(2,1)S(1)}, u32[]{:S(2)}, u32[]{:S(2)}) %all-to-all-start) | async-done | bytes 416 | tf_op jit(solution)/shard_map/all_to_all | solution.py:43
  39.2 7.2 %all-to-all-start.1 = ((bf16[64,3,4096]{2,1,0:T(4,128)(2,1)}), bf16[64,3,4096]{2,1,0:T(4,128)(2,1)}, u32[]{:S(2)}, u32[]{:S(2)}) async-start(bf16[64,3,4096]{2,1,0:T(4,128)(2,1)} %reshape.56), calls=%async_computation.1 | async-start | bytes 4194304 | tf_op jit(solution)/shard_map/all_to_all | solution.py:36
  46.4 0.0 copy-done.1
  46.4 0.0 copy-done.3
  46.4 0.2 convolution_convert_fusion.1
  46.6 5.9 %fusion = f32[192,4096]{1,0:T(8,128)} fusion(bf16[1,768,4096]{2,1,0:T(8,128)(2,1)} %param.11, bf16[1,1,192,768]{3,2,1,0:T(8,128)(2,1)S(1)} %copy-done.1), kind=kOutput, calls=%fused_computation | convolution fusion | flops 1207959552 | bytes 9732096 | tf_op jit(solution)/shard_map/dot_general | solution.py:71
  52.5 0.0 copy-start.2
  52.5 0.1 convert_reduce_fusion
  52.6 0.1 reshape.60
  52.7 89.9 %all-to-all-done.1 = bf16[64,3,4096]{2,1,0:T(4,128)(2,1)} async-done(((bf16[64,3,4096]{2,1,0:T(4,128)(2,1)}), bf16[64,3,4096]{2,1,0:T(4,128)(2,1)}, u32[]{:S(2)}, u32[]{:S(2)}) %all-to-all-start.1) | async-done | bytes 1572896 | tf_op jit(solution)/shard_map/all_to_all | solution.py:36
  142.6 3.1 reshape.57
  145.8 0.0 copy-done.2
  145.8 0.6 fusion.20
  146.3 2.7 fusion.10
  149.1 0.8 all_to_all.15
  149.8 8.0 %all-to-all-start.2 = ((f32[64,1,3]{2,1,0:T(1,128)}), f32[64,1,3]{2,1,0:T(1,128)S(1)}, u32[]{:S(2)}, u32[]{:S(2)}) async-start(f32[64,1,3]{2,1,0:T(1,128)} %bitcast.7), calls=%async_computation.2 | async-start | bytes 65536 | tf_op jit(solution)/shard_map/all_to_all | solution.py:81
  157.8 0.0 all-reduce.3.cloned.1.call-start
  157.9 1.3 fusion.6
  159.2 0.8 fusion.15
  160.0 0.0 all-reduce.3.cloned.1.call-update
  160.1 5.0 %fusion.2 = f32[192,768]{1,0:T(8,128)S(1)} fusion(bf16[192,4096]{1,0:T(8,128)(2,1)S(1)} %reshape.57, bf16[1,768,4096]{2,1,0:T(8,128)(2,1)} %param.11), kind=kOutput, calls=%fused_computation.2 | convolution fusion | flops 1207959552 | bytes 8454144 | tf_op jit(solution)/shard_map/dot_general | solution.py:63
  165.1 1.0 fusion.14
  166.0 2.5 all-to-all-done.2
  168.6 0.5 broadcast.13
  169.1 0.7 reduce.7
  169.8 0.1 broadcast_in_dim.28
  169.9 0.6 select_reduce_fusion
  170.6 294.7 %all-reduce.3.cloned.1.call-done = (f32[1,32,768]{2,1,0:T(8,128)}, f32[1,32,4096]{2,1,0:T(8,128)}) async-done(((f32[1,32,768]{2,1,0:T(8,128)}, f32[1,32,4096]{2,1,0:T(8,128)}), (f32[1,32,768]{2,1,0:T(8,128)}, f32[1,32,4096]{2,1,0:T(8,128)})) %all-reduce.3.cloned.1.call-update) | async-done | bytes 622608 | tf_op jit(solution)/shard_map/psum | solution.py:18
  465.3 1.5 copy.17
  466.9 1.9 copy.18
  (1 shorter events, 0.0 us)
Async XLA Ops:
  7.2 21.3 %copy-start = (bf16[128,4096]{1,0:T(8,128)(2,1)S(1)}, bf16[128,4096]{1,0:T(8,128)(2,1)}, u32[]{:S(2)}) copy-start(bf16[128,4096]{1,0:T(8,128)(2,1)} %param.7) | copy-start | bytes 3145732
  11.3 27.9 %all-to-all-start = ((bf16[64,1,3]{2,1,0:T(2,128)(2,1)}), bf16[64,1,3]{2,1,0:T(2,128)(2,1)S(1)}, u32[]{:S(2)}, u32[]{:S(2)}) async-start(bf16[64,1,3]{2,1,0:T(2,128)(2,1)} %convert_element_type.66), calls=%async_computation | async-start | bytes 65536 | tf_op jit(solution)/shard_map/all_to_all | solution.py:43
  29.1 17.3 %copy-start.1 = (bf16[1,1,192,768]{3,2,1,0:T(8,128)(2,1)S(1)}, bf16[1,1,192,768]{3,2,1,0:T(8,128)(2,1)}, u32[]{:S(2)}) copy-start(bf16[1,1,192,768]{3,2,1,0:T(8,128)(2,1)} %param.10) | copy-start | bytes 884740
  29.1 17.3 %copy-start.3 = (bf16[1,32,768]{2,1,0:T(8,128)(2,1)S(1)}, bf16[1,32,768]{2,1,0:T(8,128)(2,1)}, u32[]{:S(2)}) copy-start(bf16[1,32,768]{2,1,0:T(8,128)(2,1)} %param.12) | copy-start | bytes 147460
  39.2 103.4 %all-to-all-start.1 = ((bf16[64,3,4096]{2,1,0:T(4,128)(2,1)}), bf16[64,3,4096]{2,1,0:T(4,128)(2,1)}, u32[]{:S(2)}, u32[]{:S(2)}) async-start(bf16[64,3,4096]{2,1,0:T(4,128)(2,1)} %reshape.56), calls=%async_computation.1 | async-start | bytes 4194304 | tf_op jit(solution)/shard_map/all_to_all | solution.py:36
  52.5 93.3 %copy-start.2 = (bf16[1,32,4096]{2,1,0:T(8,128)(2,1)S(1)}, bf16[1,32,4096]{2,1,0:T(8,128)(2,1)}, u32[]{:S(2)}) copy-start(bf16[1,32,4096]{2,1,0:T(8,128)(2,1)} %param.13) | copy-start | bytes 786436
  149.8 18.7 %all-to-all-start.2 = ((f32[64,1,3]{2,1,0:T(1,128)}), f32[64,1,3]{2,1,0:T(1,128)S(1)}, u32[]{:S(2)}, u32[]{:S(2)}) async-start(f32[64,1,3]{2,1,0:T(1,128)} %bitcast.7), calls=%async_computation.2 | async-start | bytes 65536 | tf_op jit(solution)/shard_map/all_to_all | solution.py:81
  157.8 307.5 %all-reduce.3.cloned.1.call-start = ((), (), s32[]{:S(2)}) async-start(), calls=%async_computation.3 | async-start | bytes 1245184 | tf_op jit(solution)/shard_map/psum | solution.py:18
Sparse Core Ops, SparseCore 0:
  162.8 302.4 all-reduce.2
where the time goes:
time: 478 us; the launch traced here: 476 us
  waiting for transfers between devices  395 us (83%)
  starting transfers between devices  32.4 us (7%)
  matrix products  18.9 us (4%)
  between operations  14.2 us (3%)
  local copies, waits for them, and re-layouts  11.3 us (2%)
    psum x1, waiting for transfers between devices, sum_adapters(): return lax.psum((first_factor_gradient, second_factor_gradient), 'dp')  295 us
    all_to_all x1, waiting for transfers between devices, shards(): lax.all_to_all(outgoing.reshape(experts, capacity, -1), 'expert', split_a...  89.9 us
    all_to_all x1, starting transfers between devices, shards(): lax.all_to_all(outgoing_gate.reshape(experts, capacity), 'expert', split_...  17.2 us
  transfers between devices with their start and end apart: 4, of which 4 were waited for; matrix products, arithmetic and copies ran while one was open for 4% of the time, Pallas kernels for 0%

commit v1 on v0

v1 whole, which is shorter than its diff:
```python
import jax
import jax.numpy as jnp
from jax import lax
from jax.sharding import PartitionSpec as P

adapter_scale = 2.0
Y_SIZE = 4


def dp_groups():
    z_count = lax.axis_size("dp") // Y_SIZE
    along_y = [[z * Y_SIZE + y for y in range(Y_SIZE)] for z in range(z_count)]
    along_z = [[z * Y_SIZE + y for z in range(z_count)] for y in range(Y_SIZE)]
    return along_y, along_z


def exchange(blocks, axis, groups=None):
    return lax.all_to_all(blocks, axis, split_axis=0, concat_axis=0, tiled=True, axis_index_groups=groups)


def sum_over_dp(part):
    along_y, along_z = dp_groups()
    rank, columns = part.shape
    mine = part.astype(jnp.bfloat16).reshape(Y_SIZE, rank // Y_SIZE, columns)
    summed = jnp.sum(exchange(mine, "dp", along_y).astype(jnp.float32), axis=0)
    copies = jnp.broadcast_to(summed.astype(jnp.bfloat16)[None], (len(along_z[0]),) + summed.shape)
    summed = jnp.sum(exchange(copies, "dp", along_z).astype(jnp.float32), axis=0)
    copies = jnp.broadcast_to(summed.astype(jnp.bfloat16)[None], (Y_SIZE,) + summed.shape)
    return exchange(copies, "dp", along_y).reshape(rank, columns)


def shards(grad_out, expert_ids, gate_weight, saved_hidden, down_weight, adapter_a, adapter_b):
    experts = lax.axis_size("expert")
    capacity = saved_hidden.shape[2] // experts
    slots = experts * capacity
    width = grad_out.shape[1]
    hidden_width = saved_hidden.shape[3]
    gates = gate_weight.astype(jnp.float32)
    labels = jnp.arange(experts, dtype=jnp.int32)
    onehot = (expert_ids[:, None] == labels[None, :]).astype(jnp.int32)
    token_rank = jnp.sum((jnp.cumsum(onehot, axis=0) - onehot) * onehot, axis=1)
    slot_index = expert_ids * capacity + token_rank
    chosen = jnp.arange(slots, dtype=jnp.int32)[:, None] == slot_index[None, :]
    scaled = (gates[:, None] * grad_out.astype(jnp.float32)).astype(jnp.bfloat16)
    outgoing = jnp.dot(chosen.astype(jnp.bfloat16), scaled, preferred_element_type=jnp.float32).astype(jnp.bfloat16)
    arrived = exchange(outgoing.reshape(experts, capacity * 8, width // 8), "expert")
    rows = arrived.reshape(slots, width)

    hidden = saved_hidden.reshape(slots, hidden_width)
    weight, factor_a, factor_b = down_weight[0], adapter_a[0], adapter_b[0]
    low_rank = jnp.dot(hidden, factor_a.T, preferred_element_type=jnp.float32).astype(jnp.bfloat16)
    over_columns = (((1,), (1,)), ((), ()))
    over_slots = (((0,), (0,)), ((), ()))
    adapter_proj = lax.dot_general(rows, factor_b, over_columns, preferred_element_type=jnp.float32)
    rounded_proj = adapter_proj.astype(jnp.bfloat16)
    part_b = adapter_scale * lax.dot_general(low_rank, rows, over_slots, preferred_element_type=jnp.float32)
    part_a = adapter_scale * lax.dot_general(rounded_proj, hidden, over_slots, preferred_element_type=jnp.float32)
    summed = sum_over_dp(jnp.concatenate([part_b, part_a], axis=1)).astype(jnp.float32)

    projected = lax.dot_general(rows, weight, over_columns, preferred_element_type=jnp.float32)
    back = jnp.dot(rounded_proj, factor_a, preferred_element_type=jnp.float32)
    hidden_gradient = (projected + adapter_scale * back).astype(jnp.bfloat16)
    gate_terms = jnp.sum(hidden.astype(jnp.float32) * projected, axis=1)
    gate_terms = gate_terms + adapter_scale * jnp.sum(low_rank.astype(jnp.float32) * adapter_proj, axis=1)
    came_back = exchange(gate_terms.reshape(experts, capacity), "expert").reshape(-1)
    gate_grad = jnp.sum(jnp.where(chosen, came_back[:, None], 0.0), axis=0) / gates
    return (hidden_gradient.reshape(saved_hidden.shape), gate_grad, summed[None, :, width:], summed[None, :, :width])


def solution(mesh):
    in_specs = (
        P(("dp", "expert"), None),
        P(("dp", "expert")),
        P(("dp", "expert")),
        P("dp", "expert", None, None),
        P("expert", None, None),
        P("expert", None, None),
        P("expert", None, None),
    )
    out_specs = (
        P("dp", "expert", None, None),
        P(("dp", "expert")),
        P("expert", None, None),
        P("expert", None, None),
    )
    return jax.shard_map(shards, mesh=mesh, in_specs=in_specs, out_specs=out_specs, check_vma=False)
```

time: 478 us -> 209 us (0.44)
  the two profiles are of different devices: /device:TPU:6 before, /device:TPU:32 now
where the time goes in v1:
time: 209 us; the launch traced here: 208 us
  waiting for transfers between devices  129 us (62%)
  starting transfers between devices  56.8 us (27%)
  matrix products  9.31 us (4%)
  local copies, waits for them, and re-layouts  7.26 us (3%)
  other arithmetic  5.34 us (3%)
    all_to_all x5, waiting for transfers between devices, exchange(): lax.all_to_all(blocks, axis, split_axis=0, concat_axis=0, tiled=True, axi...  129 us
    all_to_all x5, starting transfers between devices, exchange(): lax.all_to_all(blocks, axis, split_axis=0, concat_axis=0, tiled=True, axi...  56.8 us
    dot_general x1, matrix products, shards(): lax.dot_general(rows, weight, over_columns, preferred_element_type=jnp.fl...  5.1 us
  transfers between devices with their start and end apart: 5, of which 5 were waited for; matrix products, arithmetic and copies ran while one was open for 4% of the time, Pallas kernels for 0%

profile of v1, /device:TPU:32, one launch (start us, length us, event | category | flops | bytes accessed | tf_op | source)
XLA Modules:
  0.0 208.3 jit_solution(5657651735568357089)
XLA Ops:
  0.6 0.0 copy-start
  0.6 0.8 fusion.14
  1.4 0.2 reduce_window_sum.11
  1.6 0.8 select_reduce_fusion.1
  2.4 0.7 multiply_add_fusion.1
  3.1 0.7 convert_element_type.44
  3.8 1.9 convolution_convert_fusion
  5.6 2.1 %reshape.63 = bf16[64,24,512]{2,1,0:T(8,128)(2,1)} reshape(bf16[192,4096]{1,0:T(8,128)(2,1)S(1)} %convolution_convert_fusion) | data formatting | bytes 3145728 | tf_op jit(solution)/shard_map/reshape | solution.py:46
  7.8 0.0 copy-start.1
  7.8 0.0 copy-start.3
  7.8 17.0 %all-to-all-start = ((bf16[64,24,512]{2,1,0:T(8,128)(2,1)}), bf16[64,24,512]{2,1,0:T(8,128)(2,1)S(1)}, u32[]{:S(2)}, u32[]{:S(2)}) async-start(bf16[64,24,512]{2,1,0:T(8,128)(2,1)} %reshape.63), calls=%async_computation | async-start | bytes 3145728 | tf_op jit(solution)/shard_map/all_to_all | solution.py:18
  24.8 0.0 copy-done.1
  24.8 0.0 copy-done.3
  24.8 0.2 convolution_convert_fusion.1
  25.0 69.4 %all-to-all-done = bf16[64,24,512]{2,1,0:T(8,128)(2,1)S(1)} async-done(((bf16[64,24,512]{2,1,0:T(8,128)(2,1)}), bf16[64,24,512]{2,1,0:T(8,128)(2,1)S(1)}, u32[]{:S(2)}, u32[]{:S(2)}) %all-to-all-start) | async-done | bytes 1572896 | tf_op jit(solution)/shard_map/all_to_all | solution.py:18
  94.4 0.8 reshape.64
  95.2 0.0 copy-start.2
  95.2 0.4 fusion.3
  95.6 0.0 copy-done
  95.6 0.6 multiply_reduce_fusion.1
  96.2 0.0 copy-done.2
  96.2 0.2 fusion.8
  96.4 0.7 pad_maximum_fusion
  97.2 3.5 %all-to-all-start.2 = ((bf16[4,8,4864]{2,1,0:T(8,128)(2,1)}), bf16[4,8,4864]{2,1,0:T(8,128)(2,1)S(1)}, u32[]{:S(2)}, u32[]{:S(2)}) async-start(bf16[4,8,4864]{2,1,0:T(8,128)(2,1)} %pad_maximum_fusion), calls=%async_computation.2 | async-start | bytes 622592 | tf_op jit(solution)/shard_map/all_to_all | solution.py:18
  100.6 5.1 %multiply_reduce_fusion = (f32[192]{0:T(256)S(1)}, f32[192,768]{1,0:T(8,128)S(1)}) fusion(bf16[1,1,192,768]{3,2,1,0:T(8,128)(2,1)S(1)} %copy-done.2, bf16[192,4096]{1,0:T(8,128)(2,1)S(1)} %reshape.64, bf16[1,768,4096]{2,1,0:T(8,128)(2,1)} %param.11), kind=kOutput, calls=%fused_computation.16 | convolution fusion | flops 1208401664 | bytes 8749824 | tf_op jit(solution)/shard_map/dot_general | solution.py:60
  105.7 0.8 add.23
  106.5 1.4 all-to-all-done.2
  107.9 12.4 %all-to-all-start.1 = ((f32[64,1,3]{2,1,0:T(1,128)}), f32[64,1,3]{2,1,0:T(1,128)S(1)}, u32[]{:S(2)}, u32[]{:S(2)}) async-start(f32[64,1,3]{2,1,0:T(1,128)} %bitcast.5), calls=%async_computation.1 | async-start | bytes 65536 | tf_op jit(solution)/shard_map/all_to_all | solution.py:18
  120.4 11.2 %all-to-all-done.1 = f32[64,1,3]{2,1,0:T(1,128)S(1)} async-done(((f32[64,1,3]{2,1,0:T(1,128)}), f32[64,1,3]{2,1,0:T(1,128)S(1)}, u32[]{:S(2)}, u32[]{:S(2)}) %all-to-all-start.1) | async-done | bytes 800 | tf_op jit(solution)/shard_map/all_to_all | solution.py:18
  131.6 0.7 broadcast_in_dim.40
  132.3 0.0 copy-start.4
  132.3 20.1 %all-to-all-start.3 = ((bf16[4,8,4864]{2,1,0:T(8,128)(2,1)}), bf16[4,8,4864]{2,1,0:T(8,128)(2,1)S(1)}, u32[]{:S(2)}, u32[]{:S(2)}) async-start(bf16[4,8,4864]{2,1,0:T(8,128)(2,1)} %broadcast_in_dim.40), calls=%async_computation.3 | async-start | bytes 622592 | tf_op jit(solution)/shard_map/all_to_all | solution.py:18
  152.4 1.0 fusion.6
  153.4 0.5 broadcast.23
  153.9 0.7 reduce.5
  154.6 0.1 broadcast_in_dim.22
  154.8 40.1 %all-to-all-done.3 = bf16[4,8,4864]{2,1,0:T(8,128)(2,1)S(1)} async-done(((bf16[4,8,4864]{2,1,0:T(8,128)(2,1)}), bf16[4,8,4864]{2,1,0:T(8,128)(2,1)S(1)}, u32[]{:S(2)}, u32[]{:S(2)}) %all-to-all-start.3) | async-done | bytes 311328 | tf_op jit(solution)/shard_map/all_to_all | solution.py:18
  195.0 0.7 broadcast_in_dim.41
  195.7 3.7 %all-to-all-start.4 = ((bf16[4,8,4864]{2,1,0:T(8,128)(2,1)}), bf16[4,8,4864]{2,1,0:T(8,128)(2,1)S(1)}, u32[]{:S(2)}, u32[]{:S(2)}) async-start(bf16[4,8,4864]{2,1,0:T(8,128)(2,1)} %broadcast_in_dim.41), calls=%async_computation.4 | async-start | bytes 622592 | tf_op jit(solution)/shard_map/all_to_all | solution.py:18
  199.4 0.1 select_reduce_fusion
  199.5 0.0 copy-done.4
  199.5 0.5 convert_divide_fusion
  200.1 6.7 %all-to-all-done.4 = bf16[4,8,4864]{2,1,0:T(8,128)(2,1)S(1)} async-done(((bf16[4,8,4864]{2,1,0:T(8,128)(2,1)}), bf16[4,8,4864]{2,1,0:T(8,128)(2,1)S(1)}, u32[]{:S(2)}, u32[]{:S(2)}) %all-to-all-start.4) | async-done | bytes 311328 | tf_op jit(solution)/shard_map/all_to_all | solution.py:18
  206.9 0.8 slice_bitcast_fusion
  207.7 0.6 slice_bitcast_fusion.1
  (4 shorter events, 0.1 us)
Async XLA Ops:
  0.6 95.0 %copy-start = (bf16[1,32,4096]{2,1,0:T(8,128)(2,1)S(1)}, bf16[1,32,4096]{2,1,0:T(8,128)(2,1)}, u32[]{:S(2)}) copy-start(bf16[1,32,4096]{2,1,0:T(8,128)(2,1)} %param.13) | copy-start | bytes 786436
  7.8 17.1 %copy-start.1 = (bf16[1,1,192,768]{3,2,1,0:T(8,128)(2,1)S(1)}, bf16[1,1,192,768]{3,2,1,0:T(8,128)(2,1)}, u32[]{:S(2)}) copy-start(bf16[1,1,192,768]{3,2,1,0:T(8,128)(2,1)} %param.10) | copy-start | bytes 884740
  7.8 17.1 %copy-start.3 = (bf16[1,32,768]{2,1,0:T(8,128)(2,1)S(1)}, bf16[1,32,768]{2,1,0:T(8,128)(2,1)}, u32[]{:S(2)}) copy-start(bf16[1,32,768]{2,1,0:T(8,128)(2,1)} %param.12) | copy-start | bytes 147460
  7.8 86.7 %all-to-all-start = ((bf16[64,24,512]{2,1,0:T(8,128)(2,1)}), bf16[64,24,512]{2,1,0:T(8,128)(2,1)S(1)}, u32[]{:S(2)}, u32[]{:S(2)}) async-start(bf16[64,24,512]{2,1,0:T(8,128)(2,1)} %reshape.63), calls=%async_computation | async-start | bytes 3145728 | tf_op jit(solution)/shard_map/all_to_all | solution.py:18
  95.2 1.0 copy-start.2
  97.2 10.7 %all-to-all-start.2 = ((bf16[4,8,4864]{2,1,0:T(8,128)(2,1)}), bf16[4,8,4864]{2,1,0:T(8,128)(2,1)S(1)}, u32[]{:S(2)}, u32[]{:S(2)}) async-start(bf16[4,8,4864]{2,1,0:T(8,128)(2,1)} %pad_maximum_fusion), calls=%async_computation.2 | async-start | bytes 622592 | tf_op jit(solution)/shard_map/all_to_all | solution.py:18
  107.9 23.7 %all-to-all-start.1 = ((f32[64,1,3]{2,1,0:T(1,128)}), f32[64,1,3]{2,1,0:T(1,128)S(1)}, u32[]{:S(2)}, u32[]{:S(2)}) async-start(f32[64,1,3]{2,1,0:T(1,128)} %bitcast.5), calls=%async_computation.1 | async-start | bytes 65536 | tf_op jit(solution)/shard_map/all_to_all | solution.py:18
  132.3 67.2 %copy-start.4 = (bf16[128]{0:T(256)(128)(2,1)S(1)}, bf16[128]{0:T(256)(128)(2,1)}, u32[]{:S(2)}) copy-start(bf16[128]{0:T(256)(128)(2,1)} %param.9) | copy-start | bytes 772
  132.3 62.6 %all-to-all-start.3 = ((bf16[4,8,4864]{2,1,0:T(8,128)(2,1)}), bf16[4,8,4864]{2,1,0:T(8,128)(2,1)S(1)}, u32[]{:S(2)}, u32[]{:S(2)}) async-start(bf16[4,8,4864]{2,1,0:T(8,128)(2,1)} %broadcast_in_dim.40), calls=%async_computation.3 | async-start | bytes 622592 | tf_op jit(solution)/shard_map/all_to_all | solution.py:18
  195.7 11.1 %all-to-all-start.4 = ((bf16[4,8,4864]{2,1,0:T(8,128)(2,1)}), bf16[4,8,4864]{2,1,0:T(8,128)(2,1)S(1)}, u32[]{:S(2)}, u32[]{:S(2)}) async-start(bf16[4,8,4864]{2,1,0:T(8,128)(2,1)} %broadcast_in_dim.41), calls=%async_computation.4 | async-start | bytes 622592 | tf_op jit(solution)/shard_map/all_to_all | solution.py:18

commit v2 on v1

--- a/solution.py
+++ b/solution.py
@@ -7,26 +7,49 @@
 Y_SIZE = 4
 
 
-def dp_groups():
-    z_count = lax.axis_size("dp") // Y_SIZE
-    along_y = [[z * Y_SIZE + y for y in range(Y_SIZE)] for z in range(z_count)]
-    along_z = [[z * Y_SIZE + y for z in range(z_count)] for y in range(Y_SIZE)]
-    return along_y, along_z
-
-
 def exchange(blocks, axis, groups=None):
     return lax.all_to_all(blocks, axis, split_axis=0, concat_axis=0, tiled=True, axis_index_groups=groups)
 
 
-def sum_over_dp(part):
-    along_y, along_z = dp_groups()
-    rank, columns = part.shape
-    mine = part.astype(jnp.bfloat16).reshape(Y_SIZE, rank // Y_SIZE, columns)
-    summed = jnp.sum(exchange(mine, "dp", along_y).astype(jnp.float32), axis=0)
-    copies = jnp.broadcast_to(summed.astype(jnp.bfloat16)[None], (len(along_z[0]),) + summed.shape)
-    summed = jnp.sum(exchange(copies, "dp", along_z).astype(jnp.float32), axis=0)
-    copies = jnp.broadcast_to(summed.astype(jnp.bfloat16)[None], (Y_SIZE,) + summed.shape)
-    return exchange(copies, "dp", along_y).reshape(rank, columns)
+def y_groups():
+    z_count = lax.axis_size("dp") // Y_SIZE
+    return [[z * Y_SIZE + y for y in range(Y_SIZE)] for z in range(z_count)]
+
+
+def narrow(values):
+    return lax.reduce_precision(values, exponent_bits=8, mantissa_bits=7)
+
+
+def head_and_rest(values, split):
+    tail = values[:, split:]
+    head = narrow(tail)
+    return jnp.concatenate([narrow(values[:, :split]), head, narrow(tail - head)], axis=1)
+
+
+def joined(values, split):
+    middle = split + (values.shape[1] - split) // 2
+    return jnp.concatenate([values[:, :split], values[:, split:middle] + values[:, middle:]], axis=1)
+
+
+def sum_over_y(part, split):
+    rank = part.shape[0]
+    mine = head_and_rest(part, split).astype(jnp.bfloat16).reshape(Y_SIZE, rank // Y_SIZE, -1)
+    return joined(jnp.sum(exchange(mine, "dp", y_groups()).astype(jnp.float32), axis=0), split)
+
+
+def sum_over_z(part, split):
+    z_count = lax.axis_size("dp") // Y_SIZE
+    for mask in (1, z_count - 1):
+        pairs = [(z * Y_SIZE + y, (z ^ mask) * Y_SIZE + y) for z in range(z_count) for y in range(Y_SIZE)]
+        own = head_and_rest(part, split)
+        other = lax.ppermute(own.astype(jnp.bfloat16), "dp", pairs)
+        part = joined(own + other.astype(jnp.float32), split)
+    return part
+
+
+def gather_over_y(part):
+    copies = jnp.broadcast_to(part.astype(jnp.bfloat16)[None], (Y_SIZE,) + part.shape)
+    return exchange(copies, "dp", y_groups()).reshape(-1, part.shape[1])
 
 
 def shards(grad_out, expert_ids, gate_weight, saved_hidden, down_weight, adapter_a, adapter_b):
@@ -55,13 +78,15 @@
     rounded_proj = adapter_proj.astype(jnp.bfloat16)
     part_b = adapter_scale * lax.dot_general(low_rank, rows, over_slots, preferred_element_type=jnp.float32)
     part_a = adapter_scale * lax.dot_general(rounded_proj, hidden, over_slots, preferred_element_type=jnp.float32)
-    summed = sum_over_dp(jnp.concatenate([part_b, part_a], axis=1)).astype(jnp.float32)
+    over_y = sum_over_y(jnp.concatenate([part_b, part_a], axis=1), width)
+    summed = gather_over_y(sum_over_z(over_y, width)).astype(jnp.float32)
 
     projected = lax.dot_general(rows, weight, over_columns, preferred_element_type=jnp.float32)
     back = jnp.dot(rounded_proj, factor_a, preferred_element_type=jnp.float32)
     hidden_gradient = (projected + adapter_scale * back).astype(jnp.bfloat16)
     gate_terms = jnp.sum(hidden.astype(jnp.float32) * projected, axis=1)
     gate_terms = gate_terms + adapter_scale * jnp.sum(low_rank.astype(jnp.float32) * adapter_proj, axis=1)
+    gate_terms, _ = lax.optimization_barrier((gate_terms, over_y))
     came_back = exchange(gate_terms.reshape(experts, capacity), "expert").reshape(-1)
     gate_grad = jnp.sum(jnp.where(chosen, came_back[:, None], 0.0), axis=0) / gates
     return (hidden_gradient.reshape(saved_hidden.shape), gate_grad, summed[None, :, width:], summed[None, :, :width])

time: 209 us -> 177 us (0.85)
  the two profiles are of different devices: /device:TPU:32 before, /device:TPU:6 now
where the time goes in v2:
time: 177 us; the launch traced here: 176 us
  waiting for transfers between devices  99.1 us (56%)
  starting transfers between devices  54.9 us (31%)
  matrix products  9.31 us (5%)
  local copies, waits for them, and re-layouts  6.53 us (4%)
  other arithmetic  5.42 us (3%)
    all_to_all x4, waiting for transfers between devices, exchange(): lax.all_to_all(blocks, axis, split_axis=0, concat_axis=0, tiled=True, axi...  83 us
    all_to_all x4, starting transfers between devices, exchange(): lax.all_to_all(blocks, axis, split_axis=0, concat_axis=0, tiled=True, axi...  32.5 us
    ppermute x2, starting transfers between devices, sum_over_z(): other = lax.ppermute(own.astype(jnp.bfloat16), 'dp', pairs)  22.5 us
    ppermute x2, waiting for transfers between devices, sum_over_z(): other = lax.ppermute(own.astype(jnp.bfloat16), 'dp', pairs)  16.1 us
    dot_general x1, matrix products, shards(): lax.dot_general(rows, weight, over_columns, preferred_element_type=jnp.fl...  5.1 us
  transfers between devices with their start and end apart: 6, of which 5 were waited for; matrix products, arithmetic and copies ran while one was open for 5% of the time, Pallas kernels for 0%

profile of v2, /device:TPU:6, one launch (start us, length us, event | category | flops | bytes accessed | tf_op | source)
XLA Modules:
  0.0 176.2 jit_solution(4267171984810469882)
XLA Ops:
  0.6 0.0 copy-start
  0.6 0.8 fusion.17
  1.4 0.2 reduce_window_sum.11
  1.6 0.8 select_reduce_fusion.1
  2.4 0.7 multiply_add_fusion.1
  3.1 0.7 convert_element_type.60
  3.8 1.9 %convolution_convert_fusion = bf16[192,4096]{1,0:T(8,128)(2,1)S(1)} fusion(bf16[128,4096]{1,0:T(8,128)(2,1)} %param.7, f32[128]{0:T(128)S(1)} %convert_element_type.60, s32[128]{0:T(128)S(1)} %multiply_add_fusion.1), kind=kOutput, calls=%fused_computation.2 | convolution fusion | flops 203710464 | bytes 2622464 | tf_op jit(solution)/shard_map/dot_general | solution.py:68
  5.6 2.1 %reshape.54 = bf16[64,24,512]{2,1,0:T(8,128)(2,1)} reshape(bf16[192,4096]{1,0:T(8,128)(2,1)S(1)} %convolution_convert_fusion) | data formatting | bytes 3145728 | tf_op jit(solution)/shard_map/reshape | solution.py:69
  7.7 0.0 copy-start.1
  7.8 0.0 copy-start.3
  7.8 17.4 %all-to-all-start = ((bf16[64,24,512]{2,1,0:T(8,128)(2,1)}), bf16[64,24,512]{2,1,0:T(8,128)(2,1)S(1)}, u32[]{:S(2)}, u32[]{:S(2)}) async-start(bf16[64,24,512]{2,1,0:T(8,128)(2,1)} %reshape.54), calls=%async_computation | async-start | bytes 3145728 | tf_op jit(solution)/shard_map/all_to_all | solution.py:11
  25.2 0.0 copy-done.1
  25.2 0.0 copy-done.3
  25.2 0.2 convolution_convert_fusion.1
  25.4 73.6 %all-to-all-done = bf16[64,24,512]{2,1,0:T(8,128)(2,1)S(1)} async-done(((bf16[64,24,512]{2,1,0:T(8,128)(2,1)}), bf16[64,24,512]{2,1,0:T(8,128)(2,1)S(1)}, u32[]{:S(2)}, u32[]{:S(2)}) %all-to-all-start) | async-done | bytes 1572896 | tf_op jit(solution)/shard_map/all_to_all | solution.py:11
  99.0 0.8 reshape.55
  99.8 0.0 copy-start.2
  99.8 0.4 fusion.4
  100.2 0.0 copy-done
  100.2 0.6 multiply_reduce_fusion.1
  100.8 0.0 copy-done.2
  100.8 0.2 fusion.19
  101.0 0.8 pad_maximum_fusion
  101.8 3.5 %all-to-all-start.2 = ((bf16[4,8,5632]{2,1,0:T(8,128)(2,1)}), bf16[4,8,5632]{2,1,0:T(8,128)(2,1)S(1)}, u32[]{:S(2)}, u32[]{:S(2)}) async-start(bf16[4,8,5632]{2,1,0:T(8,128)(2,1)} %pad_maximum_fusion), calls=%async_computation.2 | async-start | bytes 720896 | tf_op jit(solution)/shard_map/all_to_all | solution.py:11
  105.2 5.1 %multiply_reduce_fusion = (f32[192]{0:T(256)S(1)}, f32[192,768]{1,0:T(8,128)S(1)}) fusion(bf16[1,1,192,768]{3,2,1,0:T(8,128)(2,1)S(1)} %copy-done.2, bf16[192,4096]{1,0:T(8,128)(2,1)S(1)} %reshape.55, bf16[1,768,4096]{2,1,0:T(8,128)(2,1)} %param.11), kind=kOutput, calls=%fused_computation.16 | convolution fusion | flops 1208401664 | bytes 8749824 | tf_op jit(solution)/shard_map/dot_general | solution.py:84
  110.3 2.4 %all-to-all-done.2 = bf16[4,8,5632]{2,1,0:T(8,128)(2,1)S(1)} async-done(((bf16[4,8,5632]{2,1,0:T(8,128)(2,1)}), bf16[4,8,5632]{2,1,0:T(8,128)(2,1)S(1)}, u32[]{:S(2)}, u32[]{:S(2)}) %all-to-all-start.2) | async-done | bytes 360480 | tf_op jit(solution)/shard_map/all_to_all | solution.py:11
  112.8 15.2 %collective-permute-start = (bf16[8,5632]{1,0:T(8,128)(2,1)S(1)}, bf16[8,5632]{1,0:T(8,128)(2,1)S(1)}, u32[]{:S(2)}, u32[]{:S(2)}) collective-permute-start(bf16[8,5632]{1,0:T(8,128)(2,1)S(1)} %fusion.14), channel_id=1, source_target_pairs={{0,256},{64,320},{128,384},{192,448},{256,0},{320,64},{384,128},{4... | collective-permute-start | bytes 270344 | tf_op jit(solution)/shard_map/ppermute | solution.py:45
  128.0 0.8 all_to_all.16
  128.7 8.2 %all-to-all-start.1 = ((f32[64,1,3]{2,1,0:T(1,128)}), f32[64,1,3]{2,1,0:T(1,128)S(1)}, u32[]{:S(2)}, u32[]{:S(2)}) async-start(f32[64,1,3]{2,1,0:T(1,128)} %bitcast.5), calls=%async_computation.1 | async-start | bytes 65536 | tf_op jit(solution)/shard_map/all_to_all | solution.py:11
  136.9 4.9 %collective-permute-done = bf16[8,5632]{1,0:T(8,128)(2,1)S(1)} collective-permute-done((bf16[8,5632]{1,0:T(8,128)(2,1)S(1)}, bf16[8,5632]{1,0:T(8,128)(2,1)S(1)}, u32[]{:S(2)}, u32[]{:S(2)}) %collective-permute-start) | collective-permute-done | bytes 90144 | tf_op jit(solution)/shard_map/ppermute | solution.py:45
  141.9 0.0 copy-start.4
  141.9 7.3 %collective-permute-start.1 = (bf16[8,5632]{1,0:T(8,128)(2,1)S(1)}, bf16[8,5632]{1,0:T(8,128)(2,1)S(1)}, u32[]{:S(2)}, u32[]{:S(2)}) collective-permute-start(bf16[8,5632]{1,0:T(8,128)(2,1)S(1)} %fusion.13), channel_id=1, source_target_pairs={{0,768},{64,832},{128,896},{192,960},{256,512},{320,576},{384,640}... | collective-permute-start | bytes 270344 | tf_op jit(solution)/shard_map/ppermute | solution.py:45
  149.2 1.0 fusion.7
  150.2 0.0 all-to-all-done.1
  150.2 0.5 broadcast.11
  150.7 0.7 reduce.3
  151.5 0.1 broadcast_in_dim.31
  151.6 11.1 %collective-permute-done.1 = bf16[8,5632]{1,0:T(8,128)(2,1)S(1)} collective-permute-done((bf16[8,5632]{1,0:T(8,128)(2,1)S(1)}, bf16[8,5632]{1,0:T(8,128)(2,1)S(1)}, u32[]{:S(2)}, u32[]{:S(2)}) %collective-permute-start.1) | collective-permute-done | bytes 90144 | tf_op jit(solution)/shard_map/ppermute | solution.py:45
  162.8 0.7 broadcast_in_dim.34
  163.6 3.5 %all-to-all-start.3 = ((bf16[4,8,4864]{2,1,0:T(8,128)(2,1)}), bf16[4,8,4864]{2,1,0:T(8,128)(2,1)S(1)}, u32[]{:S(2)}, u32[]{:S(2)}) async-start(bf16[4,8,4864]{2,1,0:T(8,128)(2,1)} %broadcast_in_dim.34), calls=%async_computation.3 | async-start | bytes 622592 | tf_op jit(solution)/shard_map/all_to_all | solution.py:11
  167.0 0.1 select_reduce_fusion
  167.1 0.0 copy-done.4
  167.1 0.5 convert_divide_fusion
  167.7 7.0 %all-to-all-done.3 = bf16[4,8,4864]{2,1,0:T(8,128)(2,1)S(1)} async-done(((bf16[4,8,4864]{2,1,0:T(8,128)(2,1)}), bf16[4,8,4864]{2,1,0:T(8,128)(2,1)S(1)}, u32[]{:S(2)}, u32[]{:S(2)}) %all-to-all-start.3) | async-done | bytes 311328 | tf_op jit(solution)/shard_map/all_to_all | solution.py:11
  174.7 0.8 slice_bitcast_fusion
  175.5 0.6 slice_bitcast_fusion.1
  (14 shorter events, 0.2 us)
Async XLA Ops:
  0.6 99.6 %copy-start = (bf16[1,32,4096]{2,1,0:T(8,128)(2,1)S(1)}, bf16[1,32,4096]{2,1,0:T(8,128)(2,1)}, u32[]{:S(2)}) copy-start(bf16[1,32,4096]{2,1,0:T(8,128)(2,1)} %param.13) | copy-start | bytes 786436
  7.7 17.4 %copy-start.1 = (bf16[1,1,192,768]{3,2,1,0:T(8,128)(2,1)S(1)}, bf16[1,1,192,768]{3,2,1,0:T(8,128)(2,1)}, u32[]{:S(2)}) copy-start(bf16[1,1,192,768]{3,2,1,0:T(8,128)(2,1)} %param.10) | copy-start | bytes 884740
  7.8 17.4 %copy-start.3 = (bf16[1,32,768]{2,1,0:T(8,128)(2,1)S(1)}, bf16[1,32,768]{2,1,0:T(8,128)(2,1)}, u32[]{:S(2)}) copy-start(bf16[1,32,768]{2,1,0:T(8,128)(2,1)} %param.12) | copy-start | bytes 147460
  7.8 91.2 %all-to-all-start = ((bf16[64,24,512]{2,1,0:T(8,128)(2,1)}), bf16[64,24,512]{2,1,0:T(8,128)(2,1)S(1)}, u32[]{:S(2)}, u32[]{:S(2)}) async-start(bf16[64,24,512]{2,1,0:T(8,128)(2,1)} %reshape.54), calls=%async_computation | async-start | bytes 3145728 | tf_op jit(solution)/shard_map/all_to_all | solution.py:11
  99.8 1.0 copy-start.2
  101.8 10.9 %all-to-all-start.2 = ((bf16[4,8,5632]{2,1,0:T(8,128)(2,1)}), bf16[4,8,5632]{2,1,0:T(8,128)(2,1)S(1)}, u32[]{:S(2)}, u32[]{:S(2)}) async-start(bf16[4,8,5632]{2,1,0:T(8,128)(2,1)} %pad_maximum_fusion), calls=%async_computation.2 | async-start | bytes 720896 | tf_op jit(solution)/shard_map/all_to_all | solution.py:11
  112.8 29.0 %collective-permute-start = (bf16[8,5632]{1,0:T(8,128)(2,1)S(1)}, bf16[8,5632]{1,0:T(8,128)(2,1)S(1)}, u32[]{:S(2)}, u32[]{:S(2)}) collective-permute-start(bf16[8,5632]{1,0:T(8,128)(2,1)S(1)} %fusion.14), channel_id=1, source_target_pairs={{0,256},{64,320},{128,384},{192,448},{256,0},{320,64},{384,128},{4... | collective-permute-start | bytes 270344 | tf_op jit(solution)/shard_map/ppermute | solution.py:45
  128.7 21.5 %all-to-all-start.1 = ((f32[64,1,3]{2,1,0:T(1,128)}), f32[64,1,3]{2,1,0:T(1,128)S(1)}, u32[]{:S(2)}, u32[]{:S(2)}) async-start(f32[64,1,3]{2,1,0:T(1,128)} %bitcast.5), calls=%async_computation.1 | async-start | bytes 65536 | tf_op jit(solution)/shard_map/all_to_all | solution.py:11
  141.9 25.2 %copy-start.4 = (bf16[128]{0:T(256)(128)(2,1)S(1)}, bf16[128]{0:T(256)(128)(2,1)}, u32[]{:S(2)}) copy-start(bf16[128]{0:T(256)(128)(2,1)} %param.9) | copy-start | bytes 772
  141.9 20.8 %collective-permute-start.1 = (bf16[8,5632]{1,0:T(8,128)(2,1)S(1)}, bf16[8,5632]{1,0:T(8,128)(2,1)S(1)}, u32[]{:S(2)}, u32[]{:S(2)}) collective-permute-start(bf16[8,5632]{1,0:T(8,128)(2,1)S(1)} %fusion.13), channel_id=1, source_target_pairs={{0,768},{64,832},{128,896},{192,960},{256,512},{320,576},{384,640}... | collective-permute-start | bytes 270344 | tf_op jit(solution)/shard_map/ppermute | solution.py:45
  163.6 11.1 %all-to-all-start.3 = ((bf16[4,8,4864]{2,1,0:T(8,128)(2,1)}), bf16[4,8,4864]{2,1,0:T(8,128)(2,1)S(1)}, u32[]{:S(2)}, u32[]{:S(2)}) async-start(bf16[4,8,4864]{2,1,0:T(8,128)(2,1)} %broadcast_in_dim.34), calls=%async_computation.3 | async-start | bytes 622592 | tf_op jit(solution)/shard_map/all_to_all | solution.py:11

commit v3 on v2

v3 whole, which is shorter than its diff:
```python
from functools import partial

import jax
import jax.numpy as jnp
from jax import lax
from jax.experimental import pallas as pl
from jax.experimental.pallas import tpu as pltpu
from jax.sharding import PartitionSpec as P

adapter_scale = 2.0
Y_SIZE = 4
SUBLANES = 8
LANES = 128
GRAD_PARTS = 4


def pack_kernel(capacity, ids_hbm, gate_hbm, grad_hbm, packed_ref, slot_ref, ids_ref, gate_ref, grad_ref, spread, sems):
    tokens, width = grad_ref.shape
    pieces, packed_rows, lanes = spread.shape
    slots = packed_rows // SUBLANES
    piece = width // SUBLANES
    small = [
        pltpu.make_async_copy(ids_hbm, ids_ref, sems.at[0]),
        pltpu.make_async_copy(gate_hbm, gate_ref, sems.at[1]),
    ]
    large = []
    for part in range(GRAD_PARTS):
        columns = pl.ds(part * (width // GRAD_PARTS), width // GRAD_PARTS)
        large.append(pltpu.make_async_copy(grad_hbm.at[:, columns], grad_ref.at[:, columns], sems.at[2 + part]))
    for copy in small + large:
        copy.start()
    for copy in small:
        copy.wait()
    ids = ids_ref[...]
    onehot = (lax.broadcasted_iota(jnp.int32, (slots // capacity, tokens), 0) == ids).astype(jnp.float32)
    earlier = lax.broadcasted_iota(jnp.int32, (tokens, tokens), 0) < lax.broadcasted_iota(jnp.int32, (tokens, tokens), 1)
    counts = jnp.dot(
        onehot.astype(jnp.bfloat16), earlier.astype(jnp.bfloat16), preferred_element_type=jnp.float32
    )
    token_rank = jnp.sum(onehot * counts, axis=0, keepdims=True).astype(jnp.int32)
    slot = ids * capacity + token_rank
    slot_ref[...] = slot
    gates = gate_ref[...].astype(jnp.float32)
    chosen = lax.broadcasted_iota(jnp.int32, (slots, tokens), 0) == slot
    select = jnp.where(chosen, gates, 0.0).astype(jnp.bfloat16)
    for j in range(SUBLANES):
        if j % (SUBLANES // GRAD_PARTS) == 0:
            large[j // (SUBLANES // GRAD_PARTS)].wait()
        rows = jnp.dot(select, grad_ref[:, j * piece : (j + 1) * piece], preferred_element_type=jnp.float32)
        for c in range(pieces):
            spread[c, pl.ds(j, slots, stride=SUBLANES), :] = rows[:, c * lanes : (c + 1) * lanes]
    for c in range(pieces):
        packed_ref[:, c * lanes : (c + 1) * lanes] = spread[c].astype(jnp.bfloat16)


def pack_rows(grad_out, expert_ids, gate_weight, slots, capacity):
    tokens, width = grad_out.shape
    piece = width // SUBLANES
    whole = pl.BlockSpec(memory_space=pltpu.VMEM)
    return pl.pallas_call(
        partial(pack_kernel, capacity),
        out_shape=(
            jax.ShapeDtypeStruct((slots * SUBLANES, piece), jnp.bfloat16),
            jax.ShapeDtypeStruct((1, tokens), jnp.int32),
        ),
        in_specs=[pl.BlockSpec(memory_space=pltpu.HBM)] * 3,
        out_specs=(whole, whole),
        scratch_shapes=[
            pltpu.VMEM((1, tokens), jnp.int32),
            pltpu.VMEM((1, tokens), jnp.bfloat16),
            pltpu.VMEM((tokens, width), jnp.bfloat16),
            pltpu.VMEM((piece // LANES, slots * SUBLANES, LANES), jnp.float32),
            pltpu.SemaphoreType.DMA((2 + GRAD_PARTS,)),
        ],
        compiler_params=pltpu.CompilerParams(vmem_limit_bytes=60 * 1024 * 1024),
        name="pack_rows",
    )(expert_ids.reshape(1, tokens), gate_weight.reshape(1, tokens), grad_out)


def exchange(blocks, axis, groups=None):
    return lax.all_to_all(blocks, axis, split_axis=0, concat_axis=0, tiled=True, axis_index_groups=groups)


def y_groups():
    z_count = lax.axis_size("dp") // Y_SIZE
    return [[z * Y_SIZE + y for y in range(Y_SIZE)] for z in range(z_count)]


def narrow(values):
    return lax.reduce_precision(values, exponent_bits=8, mantissa_bits=7)


def sum_over_y(part):
    rank = part.shape[0]
    mine = part.astype(jnp.bfloat16).reshape(Y_SIZE, rank // Y_SIZE, -1)
    return jnp.sum(exchange(mine, "dp", y_groups()).astype(jnp.float32), axis=0)


def pair_sum(part, mask):
    z_count = lax.axis_size("dp") // Y_SIZE
    pairs = [(z * Y_SIZE + y, (z ^ mask) * Y_SIZE + y) for z in range(z_count) for y in range(Y_SIZE)]
    own = narrow(part)
    other = lax.ppermute(own.astype(jnp.bfloat16), "dp", pairs)
    return own + other.astype(jnp.float32)


def gather_over_y(part):
    copies = jnp.broadcast_to(part.astype(jnp.bfloat16)[None], (Y_SIZE,) + part.shape)
    return exchange(copies, "dp", y_groups()).reshape(-1, part.shape[1])


def shards(grad_out, expert_ids, gate_weight, saved_hidden, down_weight, adapter_a, adapter_b):
    experts = lax.axis_size("expert")
    capacity = saved_hidden.shape[2] // experts
    slots = experts * capacity
    width = grad_out.shape[1]
    hidden_width = saved_hidden.shape[3]
    gates = gate_weight.astype(jnp.float32)
    packed, slot_index = pack_rows(grad_out, expert_ids, gate_weight, slots, capacity)
    arrived = exchange(packed.reshape(experts, capacity * SUBLANES, width // SUBLANES), "expert")
    rows = arrived.reshape(slots, width)

    hidden = saved_hidden.reshape(slots, hidden_width)
    weight, factor_a, factor_b = down_weight[0], adapter_a[0], adapter_b[0]
    low_rank = jnp.dot(hidden, factor_a.T, preferred_element_type=jnp.float32).astype(jnp.bfloat16)
    over_columns = (((1,), (1,)), ((), ()))
    over_slots = (((0,), (0,)), ((), ()))
    adapter_proj = lax.dot_general(rows, factor_b, over_columns, preferred_element_type=jnp.float32)
    rounded_proj = adapter_proj.astype(jnp.bfloat16)
    part_b = adapter_scale * lax.dot_general(low_rank, rows, over_slots, preferred_element_type=jnp.float32)
    proj_head = narrow(adapter_proj)
    both = jnp.concatenate([proj_head, narrow(adapter_proj - proj_head)], axis=1).astype(jnp.bfloat16)
    both = lax.dot_general(both, hidden, over_slots, preferred_element_type=jnp.float32)
    part_a = adapter_scale * (both[: factor_a.shape[0]] + both[factor_a.shape[0] :])
    over_y = sum_over_y(jnp.concatenate([part_b, part_a], axis=1))
    half_z = pair_sum(over_y, 1)
    summed = gather_over_y(pair_sum(half_z, lax.axis_size("dp") // Y_SIZE - 1)).astype(jnp.float32)

    projected = lax.dot_general(rows, weight, over_columns, preferred_element_type=jnp.float32)
    back = jnp.dot(rounded_proj, factor_a, preferred_element_type=jnp.float32)
    hidden_gradient = (projected + adapter_scale * back).astype(jnp.bfloat16)
    gate_terms = jnp.sum(hidden.astype(jnp.float32) * projected, axis=1)
    gate_terms = gate_terms + adapter_scale * jnp.sum(low_rank.astype(jnp.float32) * adapter_proj, axis=1)
    gate_terms, _ = lax.optimization_barrier((gate_terms, over_y))
    came_back = exchange(gate_terms.reshape(experts, capacity), "expert").reshape(-1)
    chosen = jnp.arange(slots, dtype=jnp.int32)[:, None] == slot_index
    gate_grad = jnp.sum(jnp.where(chosen, came_back[:, None], 0.0), axis=0) / gates
    return (hidden_gradient.reshape(saved_hidden.shape), gate_grad, summed[None, :, width:], summed[None, :, :width])


def solution(mesh):
    in_specs = (
        P(("dp", "expert"), None),
        P(("dp", "expert")),
        P(("dp", "expert")),
        P("dp", "expert", None, None),
        P("expert", None, None),
        P("expert", None, None),
        P("expert", None, None),
    )
    out_specs = (
        P("dp", "expert", None, None),
        P(("dp", "expert")),
        P("expert", None, None),
        P("expert", None, None),
    )
    return jax.shard_map(shards, mesh=mesh, in_specs=in_specs, out_specs=out_specs, check_vma=False)
```

time: 177 us -> 171 us (0.966)
  Pallas kernels: 0 us -> 3.88 us
  waiting for transfers between devices: 99.1 us -> 95.4 us
  other arithmetic: 5.42 us -> 2.27 us
  local copies, waits for them, and re-layouts: 6.53 us -> 4.42 us
  matrix products: 9.31 us -> 7.43 us
    pallas_call x0 -> x1, Pallas kernels: none -> 3.88 us  [pack_rows(): pl.pallas_call(partial(pack_kernel, capacity), out_shape=(jax.ShapeDtypeS...]
    ppermute x2, waiting for transfers between devices: 16.1 us -> 12.9 us  [pair_sum(): other = lax.ppermute(own.astype(jnp.bfloat16), 'dp', pairs)]
    reshape x1 -> x0, local copies, waits for them, and re-layouts: 2.11 us -> none  [shards(): outgoing.reshape(experts, capacity * 8, width // 8)]
    dot_general x2 -> x1, matrix products: 2.05 us -> 0.18 us  [shards(): lax.dot_general(both, hidden, over_slots, preferred_element_type=jnp.floa...]
where the time goes in v3:
time: 171 us; the launch traced here: 169 us
  waiting for transfers between devices  95.4 us (56%)
  starting transfers between devices  55.1 us (32%)
  matrix products  7.43 us (4%)
  local copies, waits for them, and re-layouts  4.42 us (3%)
  Pallas kernels  3.88 us (2%)
  other arithmetic  2.27 us (1%)
    all_to_all x4, waiting for transfers between devices, exchange(): lax.all_to_all(blocks, axis, split_axis=0, concat_axis=0, tiled=True, axi...  82.5 us
    all_to_all x4, starting transfers between devices, exchange(): lax.all_to_all(blocks, axis, split_axis=0, concat_axis=0, tiled=True, axi...  32.3 us
    ppermute x2, starting transfers between devices, pair_sum(): other = lax.ppermute(own.astype(jnp.bfloat16), 'dp', pairs)  22.8 us
    ppermute x2, waiting for transfers between devices, pair_sum(): other = lax.ppermute(own.astype(jnp.bfloat16), 'dp', pairs)  12.9 us
    dot_general x1, matrix products, shards(): lax.dot_general(rows, weight, over_columns, preferred_element_type=jnp.fl...  5.1 us
    pallas_call x1, Pallas kernels, pack_rows(): pl.pallas_call(partial(pack_kernel, capacity), out_shape=(jax.ShapeDtypeS...  3.88 us
  transfers between devices with their start and end apart: 6, of which 5 were waited for; matrix products, arithmetic and copies ran while one was open for 5% of the time, Pallas kernels for 0%

profile of v3, /device:TPU:6, one launch (start us, length us, event | category | flops | bytes accessed | tf_op | source)
XLA Modules:
  0.0 169.4 jit_solution(17606642133951460509)
XLA Ops:
  0.6 0.0 copy-start
  0.6 3.9 %pack_rows.1 = (bf16[1536,512]{1,0:T(8,128)(2,1)}, s32[1,128]{1,0:T(1,128)}) custom-call(s32[1,128]{1,0:T(1,128)} %bitcast.45, bf16[1,128]{1,0:T(2,128)(2,1)} %bitcast.46, bf16[128,4096]{1,0:T(8,128)(2,1)} %grad_hbm.1), custom_call_target="tpu_custom_call" | custom-call | tf_op jit(solution)/shard_map/pack_rows/pallas_call | solution.py:60
  4.5 0.0 copy-start.1
  4.5 0.0 copy-start.3
  4.6 17.4 %all-to-all-start = ((bf16[64,24,512]{2,1,0:T(8,128)(2,1)}), bf16[64,24,512]{2,1,0:T(8,128)(2,1)S(1)}, u32[]{:S(2)}, u32[]{:S(2)}) async-start(bf16[64,24,512]{2,1,0:T(8,128)(2,1)} %bitcast.44), calls=%async_computation | async-start | bytes 3145728 | tf_op jit(solution)/shard_map/all_to_all | solution.py:81
  22.0 0.0 copy-done.1
  22.0 0.0 copy-done.3
  22.0 0.2 convolution_convert_fusion
  22.2 73.6 %all-to-all-done = bf16[64,24,512]{2,1,0:T(8,128)(2,1)S(1)} async-done(((bf16[64,24,512]{2,1,0:T(8,128)(2,1)}), bf16[64,24,512]{2,1,0:T(8,128)(2,1)S(1)}, u32[]{:S(2)}, u32[]{:S(2)}) %all-to-all-start) | async-done | bytes 1572896 | tf_op jit(solution)/shard_map/all_to_all | solution.py:81
  95.8 0.8 reshape.44
  96.6 0.0 copy-start.2
  96.6 0.4 fusion.3
  97.0 0.0 copy-done
  97.0 0.6 reduce-precision_convert_fusion.1
  97.6 0.0 copy-done.2
  97.6 0.2 fusion.7
  97.8 0.7 pad_maximum_fusion
  98.6 3.5 %all-to-all-start.1 = ((bf16[4,8,4864]{2,1,0:T(8,128)(2,1)}), bf16[4,8,4864]{2,1,0:T(8,128)(2,1)S(1)}, u32[]{:S(2)}, u32[]{:S(2)}) async-start(bf16[4,8,4864]{2,1,0:T(8,128)(2,1)} %pad_maximum_fusion), calls=%async_computation.1 | async-start | bytes 622592 | tf_op jit(solution)/shard_map/all_to_all | solution.py:81
  102.0 5.1 %multiply_reduce_fusion = (f32[192]{0:T(256)S(1)}, f32[192,768]{1,0:T(8,128)S(1)}) fusion(bf16[1,1,192,768]{3,2,1,0:T(8,128)(2,1)S(1)} %copy-done.2, bf16[192,4096]{1,0:T(8,128)(2,1)S(1)} %reshape.44, bf16[1,768,4096]{2,1,0:T(8,128)(2,1)} %param.11), kind=kOutput, calls=%fused_computation.11 | convolution fusion | flops 1208401664 | bytes 8749824 | tf_op jit(solution)/shard_map/dot_general | solution.py:139
  107.1 1.8 %all-to-all-done.1 = bf16[4,8,4864]{2,1,0:T(8,128)(2,1)S(1)} async-done(((bf16[4,8,4864]{2,1,0:T(8,128)(2,1)}), bf16[4,8,4864]{2,1,0:T(8,128)(2,1)S(1)}, u32[]{:S(2)}, u32[]{:S(2)}) %all-to-all-start.1) | async-done | bytes 311328 | tf_op jit(solution)/shard_map/all_to_all | solution.py:81
  109.0 0.0 copy-start.5
  109.0 0.0 copy-start.4
  109.1 15.4 %collective-permute-start = (bf16[8,4864]{1,0:T(8,128)(2,1)S(1)}, bf16[8,4864]{1,0:T(8,128)(2,1)S(1)}, u32[]{:S(2)}, u32[]{:S(2)}) collective-permute-start(bf16[8,4864]{1,0:T(8,128)(2,1)S(1)} %reduce-precision_convert_fusion), channel_id=1, source_target_pairs={{0,256},{64,320},{128,384},{192,448},{256,0},{320,64},{384,128},{4... | collective-permute-start | bytes 233480 | tf_op jit(solution)/shard_map/ppermute | solution.py:103
  124.5 0.8 all_to_all.17
  125.2 8.0 %all-to-all-start.2 = ((f32[64,1,3]{2,1,0:T(1,128)}), f32[64,1,3]{2,1,0:T(1,128)S(1)}, u32[]{:S(2)}, u32[]{:S(2)}) async-start(f32[64,1,3]{2,1,0:T(1,128)} %bitcast.11), calls=%async_computation.2 | async-start | bytes 65536 | tf_op jit(solution)/shard_map/all_to_all | solution.py:81
  133.2 2.7 %collective-permute-done = bf16[8,4864]{1,0:T(8,128)(2,1)S(1)} collective-permute-done((bf16[8,4864]{1,0:T(8,128)(2,1)S(1)}, bf16[8,4864]{1,0:T(8,128)(2,1)S(1)}, u32[]{:S(2)}, u32[]{:S(2)}) %collective-permute-start) | collective-permute-done | bytes 77856 | tf_op jit(solution)/shard_map/ppermute | solution.py:103
  135.9 7.4 %collective-permute-start.1 = (bf16[8,4864]{1,0:T(8,128)(2,1)S(1)}, bf16[8,4864]{1,0:T(8,128)(2,1)S(1)}, u32[]{:S(2)}, u32[]{:S(2)}) collective-permute-start(bf16[8,4864]{1,0:T(8,128)(2,1)S(1)} %fusion.14), channel_id=1, source_target_pairs={{0,768},{64,832},{128,896},{192,960},{256,512},{320,576},{384,640}... | collective-permute-start | bytes 233480 | tf_op jit(solution)/shard_map/ppermute | solution.py:103
  143.4 1.0 fusion.6
  144.4 0.0 all-to-all-done.2
  144.4 0.5 broadcast.4
  144.9 0.7 reduce.3
  145.6 0.1 broadcast_in_dim.27
  145.8 10.2 %collective-permute-done.1 = bf16[8,4864]{1,0:T(8,128)(2,1)S(1)} collective-permute-done((bf16[8,4864]{1,0:T(8,128)(2,1)S(1)}, bf16[8,4864]{1,0:T(8,128)(2,1)S(1)}, u32[]{:S(2)}, u32[]{:S(2)}) %collective-permute-start.1) | collective-permute-done | bytes 77856 | tf_op jit(solution)/shard_map/ppermute | solution.py:103
  156.0 0.7 broadcast_in_dim.30
  156.8 3.5 %all-to-all-start.3 = ((bf16[4,8,4864]{2,1,0:T(8,128)(2,1)}), bf16[4,8,4864]{2,1,0:T(8,128)(2,1)S(1)}, u32[]{:S(2)}, u32[]{:S(2)}) async-start(bf16[4,8,4864]{2,1,0:T(8,128)(2,1)} %broadcast_in_dim.30), calls=%async_computation.3 | async-start | bytes 622592 | tf_op jit(solution)/shard_map/all_to_all | solution.py:81
  160.2 0.0 copy-done.5
  160.3 0.1 select_reduce_fusion
  160.4 0.0 copy-done.4
  160.4 0.5 convert_divide_fusion
  160.9 7.0 %all-to-all-done.3 = bf16[4,8,4864]{2,1,0:T(8,128)(2,1)S(1)} async-done(((bf16[4,8,4864]{2,1,0:T(8,128)(2,1)}), bf16[4,8,4864]{2,1,0:T(8,128)(2,1)S(1)}, u32[]{:S(2)}, u32[]{:S(2)}) %all-to-all-start.3) | async-done | bytes 311328 | tf_op jit(solution)/shard_map/all_to_all | solution.py:81
  167.9 0.8 slice_bitcast_fusion
  168.7 0.6 slice_bitcast_fusion.1
  (7 shorter events, 0.2 us)
Async XLA Ops:
  0.6 96.4 %copy-start = (bf16[1,32,4096]{2,1,0:T(8,128)(2,1)S(1)}, bf16[1,32,4096]{2,1,0:T(8,128)(2,1)}, u32[]{:S(2)}) copy-start(bf16[1,32,4096]{2,1,0:T(8,128)(2,1)} %param.13) | copy-start | bytes 786436
  4.5 17.4 %copy-start.1 = (bf16[1,1,192,768]{3,2,1,0:T(8,128)(2,1)S(1)}, bf16[1,1,192,768]{3,2,1,0:T(8,128)(2,1)}, u32[]{:S(2)}) copy-start(bf16[1,1,192,768]{3,2,1,0:T(8,128)(2,1)} %param.10) | copy-start | bytes 884740
  4.5 17.4 %copy-start.3 = (bf16[1,32,768]{2,1,0:T(8,128)(2,1)S(1)}, bf16[1,32,768]{2,1,0:T(8,128)(2,1)}, u32[]{:S(2)}) copy-start(bf16[1,32,768]{2,1,0:T(8,128)(2,1)} %param.12) | copy-start | bytes 147460
  4.6 91.3 %all-to-all-start = ((bf16[64,24,512]{2,1,0:T(8,128)(2,1)}), bf16[64,24,512]{2,1,0:T(8,128)(2,1)S(1)}, u32[]{:S(2)}, u32[]{:S(2)}) async-start(bf16[64,24,512]{2,1,0:T(8,128)(2,1)} %bitcast.44), calls=%async_computation | async-start | bytes 3145728 | tf_op jit(solution)/shard_map/all_to_all | solution.py:81
  96.6 1.0 copy-start.2
  98.6 10.4 %all-to-all-start.1 = ((bf16[4,8,4864]{2,1,0:T(8,128)(2,1)}), bf16[4,8,4864]{2,1,0:T(8,128)(2,1)S(1)}, u32[]{:S(2)}, u32[]{:S(2)}) async-start(bf16[4,8,4864]{2,1,0:T(8,128)(2,1)} %pad_maximum_fusion), calls=%async_computation.1 | async-start | bytes 622592 | tf_op jit(solution)/shard_map/all_to_all | solution.py:81
  109.0 51.2 %copy-start.5 = (s32[1,128]{1,0:T(1,128)S(1)}, s32[1,128]{1,0:T(1,128)}, u32[]{:S(2)}) copy-start(s32[1,128]{1,0:T(1,128)} %get-tuple-element.8) | copy-start | bytes 1540
  109.0 51.3 %copy-start.4 = (bf16[128]{0:T(256)(128)(2,1)S(1)}, bf16[128]{0:T(256)(128)(2,1)}, u32[]{:S(2)}) copy-start(bf16[128]{0:T(256)(128)(2,1)} %param.9) | copy-start | bytes 772
  109.1 26.8 %collective-permute-start = (bf16[8,4864]{1,0:T(8,128)(2,1)S(1)}, bf16[8,4864]{1,0:T(8,128)(2,1)S(1)}, u32[]{:S(2)}, u32[]{:S(2)}) collective-permute-start(bf16[8,4864]{1,0:T(8,128)(2,1)S(1)} %reduce-precision_convert_fusion), channel_id=1, source_target_pairs={{0,256},{64,320},{128,384},{192,448},{256,0},{320,64},{384,128},{4... | collective-permute-start | bytes 233480 | tf_op jit(solution)/shard_map/ppermute | solution.py:103
  125.2 19.1 %all-to-all-start.2 = ((f32[64,1,3]{2,1,0:T(1,128)}), f32[64,1,3]{2,1,0:T(1,128)S(1)}, u32[]{:S(2)}, u32[]{:S(2)}) async-start(f32[64,1,3]{2,1,0:T(1,128)} %bitcast.11), calls=%async_computation.2 | async-start | bytes 65536 | tf_op jit(solution)/shard_map/all_to_all | solution.py:81
  135.9 20.0 %collective-permute-start.1 = (bf16[8,4864]{1,0:T(8,128)(2,1)S(1)}, bf16[8,4864]{1,0:T(8,128)(2,1)S(1)}, u32[]{:S(2)}, u32[]{:S(2)}) collective-permute-start(bf16[8,4864]{1,0:T(8,128)(2,1)S(1)} %fusion.14), channel_id=1, source_target_pairs={{0,768},{64,832},{128,896},{192,960},{256,512},{320,576},{384,640}... | collective-permute-start | bytes 233480 | tf_op jit(solution)/shard_map/ppermute | solution.py:103
  156.8 11.1 %all-to-all-start.3 = ((bf16[4,8,4864]{2,1,0:T(8,128)(2,1)}), bf16[4,8,4864]{2,1,0:T(8,128)(2,1)S(1)}, u32[]{:S(2)}, u32[]{:S(2)}) async-start(bf16[4,8,4864]{2,1,0:T(8,128)(2,1)} %broadcast_in_dim.30), calls=%async_computation.3 | async-start | bytes 622592 | tf_op jit(solution)/shard_map/all_to_all | solution.py:81

commit v4 on v3

--- a/solution.py
+++ b/solution.py
@@ -96,11 +96,16 @@
     return jnp.sum(exchange(mine, "dp", y_groups()).astype(jnp.float32), axis=0)
 
 
-def pair_sum(part, mask):
-    z_count = lax.axis_size("dp") // Y_SIZE
-    pairs = [(z * Y_SIZE + y, (z ^ mask) * Y_SIZE + y) for z in range(z_count) for y in range(Y_SIZE)]
+def pair_sum(part, masks):
+    replicas, experts = lax.axis_size("dp"), lax.axis_size("expert")
+    pairs = []
+    for replica in range(replicas):
+        z, y = divmod(replica, Y_SIZE)
+        for expert in range(experts):
+            partner = (z ^ masks[expert % 2]) * Y_SIZE + y
+            pairs.append((replica * experts + expert, partner * experts + expert))
     own = narrow(part)
-    other = lax.ppermute(own.astype(jnp.bfloat16), "dp", pairs)
+    other = lax.ppermute(own.astype(jnp.bfloat16), ("dp", "expert"), pairs)
     return own + other.astype(jnp.float32)
 
 
@@ -133,8 +138,9 @@
     both = lax.dot_general(both, hidden, over_slots, preferred_element_type=jnp.float32)
     part_a = adapter_scale * (both[: factor_a.shape[0]] + both[factor_a.shape[0] :])
     over_y = sum_over_y(jnp.concatenate([part_b, part_a], axis=1))
-    half_z = pair_sum(over_y, 1)
-    summed = gather_over_y(pair_sum(half_z, lax.axis_size("dp") // Y_SIZE - 1)).astype(jnp.float32)
+    near, far = 1, lax.axis_size("dp") // Y_SIZE - 1
+    half_z = pair_sum(over_y, (near, far))
+    summed = gather_over_y(pair_sum(half_z, (far, near))).astype(jnp.float32)
 
     projected = lax.dot_general(rows, weight, over_columns, preferred_element_type=jnp.float32)
     back = jnp.dot(rounded_proj, factor_a, preferred_element_type=jnp.float32)

time: 171 us -> 165 us (0.965)
  the two profiles are of different devices: /device:TPU:6 before, /device:TPU:133 now
where the time goes in v4:
time: 165 us
  waiting for transfers between devices  87.4 us (53%)
  starting transfers between devices  58.4 us (35%)
  matrix products  7.43 us (5%)
  local copies, waits for them, and re-layouts  4.42 us (3%)
  Pallas kernels  3.88 us (2%)
  other arithmetic  2.27 us (1%)
    all_to_all x4, waiting for transfers between devices, exchange(): lax.all_to_all(blocks, axis, split_axis=0, concat_axis=0, tiled=True, axi...  75.9 us
    all_to_all x4, starting transfers between devices, exchange(): lax.all_to_all(blocks, axis, split_axis=0, concat_axis=0, tiled=True, axi...  39 us
    ppermute x2, starting transfers between devices, pair_sum(): other = lax.ppermute(own.astype(jnp.bfloat16), ('dp', 'expert'), pairs)  19.4 us
    ppermute x2, waiting for transfers between devices, pair_sum(): other = lax.ppermute(own.astype(jnp.bfloat16), ('dp', 'expert'), pairs)  11.6 us
    dot_general x1, matrix products, shards(): lax.dot_general(rows, weight, over_columns, preferred_element_type=jnp.fl...  5.1 us
    pallas_call x1, Pallas kernels, pack_rows(): pl.pallas_call(partial(pack_kernel, capacity), out_shape=(jax.ShapeDtypeS...  3.88 us
  transfers between devices with their start and end apart: 6, of which 4 were waited for; matrix products, arithmetic and copies ran while one was open for 5% of the time, Pallas kernels for 0%

profile of v4, /device:TPU:133, one launch (start us, length us, event | category | flops | bytes accessed | tf_op | source)
XLA Modules:
  0.0 164.7 jit_solution(12262879351234867021)
XLA Ops:
  0.6 0.0 copy-start
  0.6 3.9 %pack_rows.1 = (bf16[1536,512]{1,0:T(8,128)(2,1)}, s32[1,128]{1,0:T(1,128)}) custom-call(s32[1,128]{1,0:T(1,128)} %bitcast.45, bf16[1,128]{1,0:T(2,128)(2,1)} %bitcast.46, bf16[128,4096]{1,0:T(8,128)(2,1)} %grad_hbm.1), custom_call_target="tpu_custom_call" | custom-call | tf_op jit(solution)/shard_map/pack_rows/pallas_call | solution.py:60
  4.5 0.0 copy-start.1
  4.5 0.0 copy-start.3
  4.6 16.1 %all-to-all-start = ((bf16[64,24,512]{2,1,0:T(8,128)(2,1)}), bf16[64,24,512]{2,1,0:T(8,128)(2,1)S(1)}, u32[]{:S(2)}, u32[]{:S(2)}) async-start(bf16[64,24,512]{2,1,0:T(8,128)(2,1)} %bitcast.44), calls=%async_computation | async-start | bytes 3145728 | tf_op jit(solution)/shard_map/all_to_all | solution.py:81
  20.7 0.0 copy-done.1
  20.7 0.0 copy-done.3
  20.7 0.2 convolution_convert_fusion
  20.9 67.9 %all-to-all-done = bf16[64,24,512]{2,1,0:T(8,128)(2,1)S(1)} async-done(((bf16[64,24,512]{2,1,0:T(8,128)(2,1)}), bf16[64,24,512]{2,1,0:T(8,128)(2,1)S(1)}, u32[]{:S(2)}, u32[]{:S(2)}) %all-to-all-start) | async-done | bytes 1572896 | tf_op jit(solution)/shard_map/all_to_all | solution.py:81
  88.8 0.8 reshape.44
  89.5 0.0 copy-start.2
  89.5 0.4 fusion.3
  89.9 0.0 copy-done
  90.0 0.6 reduce-precision_convert_fusion.1
  90.6 0.0 copy-done.2
  90.6 0.2 fusion.7
  90.8 0.7 pad_maximum_fusion
  91.5 3.5 %all-to-all-start.1 = ((bf16[4,8,4864]{2,1,0:T(8,128)(2,1)}), bf16[4,8,4864]{2,1,0:T(8,128)(2,1)S(1)}, u32[]{:S(2)}, u32[]{:S(2)}) async-start(bf16[4,8,4864]{2,1,0:T(8,128)(2,1)} %pad_maximum_fusion), calls=%async_computation.1 | async-start | bytes 622592 | tf_op jit(solution)/shard_map/all_to_all | solution.py:81
  95.0 5.1 %multiply_reduce_fusion = (f32[192]{0:T(256)S(1)}, f32[192,768]{1,0:T(8,128)S(1)}) fusion(bf16[1,1,192,768]{3,2,1,0:T(8,128)(2,1)S(1)} %copy-done.2, bf16[192,4096]{1,0:T(8,128)(2,1)S(1)} %reshape.44, bf16[1,768,4096]{2,1,0:T(8,128)(2,1)} %param.11), kind=kOutput, calls=%fused_computation.11 | convolution fusion | flops 1208401664 | bytes 8749824 | tf_op jit(solution)/shard_map/dot_general | solution.py:145
  100.1 0.9 all-to-all-done.1
  101.1 0.0 copy-start.5
  101.1 0.0 copy-start.4
  101.1 14.0 %collective-permute-start = (bf16[8,4864]{1,0:T(8,128)(2,1)S(1)}, bf16[8,4864]{1,0:T(8,128)(2,1)S(1)}, u32[]{:S(2)}, u32[]{:S(2)}) collective-permute-start(bf16[8,4864]{1,0:T(8,128)(2,1)S(1)} %reduce-precision_convert_fusion), channel_id=1, source_target_pairs={{0,256},{1,769},{2,258},{3,771},{4,260},{5,773},{6,262},{7,775},{8... | collective-permute-start | bytes 233480 | tf_op jit(solution)/shard_map/ppermute | solution.py:108
  115.1 0.8 all_to_all.17
  115.9 16.0 %all-to-all-start.2 = ((f32[64,1,3]{2,1,0:T(1,128)}), f32[64,1,3]{2,1,0:T(1,128)S(1)}, u32[]{:S(2)}, u32[]{:S(2)}) async-start(f32[64,1,3]{2,1,0:T(1,128)} %bitcast.11), calls=%async_computation.2 | async-start | bytes 65536 | tf_op jit(solution)/shard_map/all_to_all | solution.py:81
  131.9 0.0 collective-permute-done
  131.9 5.4 %collective-permute-start.1 = (bf16[8,4864]{1,0:T(8,128)(2,1)S(1)}, bf16[8,4864]{1,0:T(8,128)(2,1)S(1)}, u32[]{:S(2)}, u32[]{:S(2)}) collective-permute-start(bf16[8,4864]{1,0:T(8,128)(2,1)S(1)} %fusion.14), channel_id=1, source_target_pairs={{0,768},{1,257},{2,770},{3,259},{4,772},{5,261},{6,774},{7,263},{8... | collective-permute-start | bytes 233480 | tf_op jit(solution)/shard_map/ppermute | solution.py:108
  137.3 1.0 fusion.6
  138.3 0.0 all-to-all-done.2
  138.3 0.5 broadcast.4
  138.8 0.7 reduce.3
  139.5 0.1 broadcast_in_dim.27
  139.7 11.6 %collective-permute-done.1 = bf16[8,4864]{1,0:T(8,128)(2,1)S(1)} collective-permute-done((bf16[8,4864]{1,0:T(8,128)(2,1)S(1)}, bf16[8,4864]{1,0:T(8,128)(2,1)S(1)}, u32[]{:S(2)}, u32[]{:S(2)}) %collective-permute-start.1) | collective-permute-done | bytes 77856 | tf_op jit(solution)/shard_map/ppermute | solution.py:108
  151.3 0.7 broadcast_in_dim.30
  152.0 3.5 %all-to-all-start.3 = ((bf16[4,8,4864]{2,1,0:T(8,128)(2,1)}), bf16[4,8,4864]{2,1,0:T(8,128)(2,1)S(1)}, u32[]{:S(2)}, u32[]{:S(2)}) async-start(bf16[4,8,4864]{2,1,0:T(8,128)(2,1)} %broadcast_in_dim.30), calls=%async_computation.3 | async-start | bytes 622592 | tf_op jit(solution)/shard_map/all_to_all | solution.py:81
  155.5 0.0 copy-done.5
  155.5 0.1 select_reduce_fusion
  155.6 0.0 copy-done.4
  155.6 0.5 convert_divide_fusion
  156.1 7.1 %all-to-all-done.3 = bf16[4,8,4864]{2,1,0:T(8,128)(2,1)S(1)} async-done(((bf16[4,8,4864]{2,1,0:T(8,128)(2,1)}), bf16[4,8,4864]{2,1,0:T(8,128)(2,1)S(1)}, u32[]{:S(2)}, u32[]{:S(2)}) %all-to-all-start.3) | async-done | bytes 311328 | tf_op jit(solution)/shard_map/all_to_all | solution.py:81
  163.2 0.8 slice_bitcast_fusion
  164.1 0.6 slice_bitcast_fusion.1
  (7 shorter events, 0.2 us)
Async XLA Ops:
  0.6 89.3 %copy-start = (bf16[1,32,4096]{2,1,0:T(8,128)(2,1)S(1)}, bf16[1,32,4096]{2,1,0:T(8,128)(2,1)}, u32[]{:S(2)}) copy-start(bf16[1,32,4096]{2,1,0:T(8,128)(2,1)} %param.13) | copy-start | bytes 786436
  4.5 16.2 %copy-start.1 = (bf16[1,1,192,768]{3,2,1,0:T(8,128)(2,1)S(1)}, bf16[1,1,192,768]{3,2,1,0:T(8,128)(2,1)}, u32[]{:S(2)}) copy-start(bf16[1,1,192,768]{3,2,1,0:T(8,128)(2,1)} %param.10) | copy-start | bytes 884740
  4.5 16.2 %copy-start.3 = (bf16[1,32,768]{2,1,0:T(8,128)(2,1)S(1)}, bf16[1,32,768]{2,1,0:T(8,128)(2,1)}, u32[]{:S(2)}) copy-start(bf16[1,32,768]{2,1,0:T(8,128)(2,1)} %param.12) | copy-start | bytes 147460
  4.6 84.2 %all-to-all-start = ((bf16[64,24,512]{2,1,0:T(8,128)(2,1)}), bf16[64,24,512]{2,1,0:T(8,128)(2,1)S(1)}, u32[]{:S(2)}, u32[]{:S(2)}) async-start(bf16[64,24,512]{2,1,0:T(8,128)(2,1)} %bitcast.44), calls=%async_computation | async-start | bytes 3145728 | tf_op jit(solution)/shard_map/all_to_all | solution.py:81
  89.5 1.0 copy-start.2
  91.5 9.5 %all-to-all-start.1 = ((bf16[4,8,4864]{2,1,0:T(8,128)(2,1)}), bf16[4,8,4864]{2,1,0:T(8,128)(2,1)S(1)}, u32[]{:S(2)}, u32[]{:S(2)}) async-start(bf16[4,8,4864]{2,1,0:T(8,128)(2,1)} %pad_maximum_fusion), calls=%async_computation.1 | async-start | bytes 622592 | tf_op jit(solution)/shard_map/all_to_all | solution.py:81
  101.1 54.4 %copy-start.5 = (s32[1,128]{1,0:T(1,128)S(1)}, s32[1,128]{1,0:T(1,128)}, u32[]{:S(2)}) copy-start(s32[1,128]{1,0:T(1,128)} %get-tuple-element.8) | copy-start | bytes 1540
  101.1 54.5 %copy-start.4 = (bf16[128]{0:T(256)(128)(2,1)S(1)}, bf16[128]{0:T(256)(128)(2,1)}, u32[]{:S(2)}) copy-start(bf16[128]{0:T(256)(128)(2,1)} %param.9) | copy-start | bytes 772
  101.1 30.8 %collective-permute-start = (bf16[8,4864]{1,0:T(8,128)(2,1)S(1)}, bf16[8,4864]{1,0:T(8,128)(2,1)S(1)}, u32[]{:S(2)}, u32[]{:S(2)}) collective-permute-start(bf16[8,4864]{1,0:T(8,128)(2,1)S(1)} %reduce-precision_convert_fusion), channel_id=1, source_target_pairs={{0,256},{1,769},{2,258},{3,771},{4,260},{5,773},{6,262},{7,775},{8... | collective-permute-start | bytes 233480 | tf_op jit(solution)/shard_map/ppermute | solution.py:108
  115.9 22.4 %all-to-all-start.2 = ((f32[64,1,3]{2,1,0:T(1,128)}), f32[64,1,3]{2,1,0:T(1,128)S(1)}, u32[]{:S(2)}, u32[]{:S(2)}) async-start(f32[64,1,3]{2,1,0:T(1,128)} %bitcast.11), calls=%async_computation.2 | async-start | bytes 65536 | tf_op jit(solution)/shard_map/all_to_all | solution.py:81
  131.9 19.3 %collective-permute-start.1 = (bf16[8,4864]{1,0:T(8,128)(2,1)S(1)}, bf16[8,4864]{1,0:T(8,128)(2,1)S(1)}, u32[]{:S(2)}, u32[]{:S(2)}) collective-permute-start(bf16[8,4864]{1,0:T(8,128)(2,1)S(1)} %fusion.14), channel_id=1, source_target_pairs={{0,768},{1,257},{2,770},{3,259},{4,772},{5,261},{6,774},{7,263},{8... | collective-permute-start | bytes 233480 | tf_op jit(solution)/shard_map/ppermute | solution.py:108
  152.0 11.2 %all-to-all-start.3 = ((bf16[4,8,4864]{2,1,0:T(8,128)(2,1)}), bf16[4,8,4864]{2,1,0:T(8,128)(2,1)S(1)}, u32[]{:S(2)}, u32[]{:S(2)}) async-start(bf16[4,8,4864]{2,1,0:T(8,128)(2,1)} %broadcast_in_dim.30), calls=%async_computation.3 | async-start | bytes 622592 | tf_op jit(solution)/shard_map/all_to_all | solution.py:81

commit v5 on v4

--- a/solution.py
+++ b/solution.py
@@ -77,6 +77,52 @@
     )(expert_ids.reshape(1, tokens), gate_weight.reshape(1, tokens), grad_out)
 
 
+def last_sum_kernel(width, own_ref, other_ref, copies_ref):
+    columns = own_ref.shape[1]
+    total = own_ref[...] + other_ref[...].astype(jnp.float32)
+    head = total.astype(jnp.bfloat16)
+    rest = (total[:, width:] - head[:, width:].astype(jnp.float32)).astype(jnp.bfloat16)
+    for copy in range(copies_ref.shape[0]):
+        copies_ref[copy, :, :columns] = head
+        copies_ref[copy, :, columns:] = rest
+
+
+def last_sum(own, other, copies, width):
+    rank, columns = own.shape
+    whole = pl.BlockSpec(memory_space=pltpu.VMEM)
+    return pl.pallas_call(
+        partial(last_sum_kernel, width),
+        out_shape=jax.ShapeDtypeStruct((copies, rank, 2 * columns - width), jnp.bfloat16),
+        in_specs=[whole] * 2,
+        out_specs=whole,
+        compiler_params=pltpu.CompilerParams(vmem_limit_bytes=8 * 1024 * 1024),
+        name="last_sum",
+    )(own, other)
+
+
+def widen_kernel(both_ref, factor_b_ref, factor_a_ref):
+    width = factor_b_ref.shape[1]
+    columns = width + factor_a_ref.shape[1]
+    factor_b_ref[...] = both_ref[:, :width].astype(jnp.float32)
+    factor_a_ref[...] = both_ref[:, width:columns].astype(jnp.float32) + both_ref[:, columns:].astype(jnp.float32)
+
+
+def widen(both, width):
+    rank, columns = both.shape
+    whole = pl.BlockSpec(memory_space=pltpu.VMEM)
+    return pl.pallas_call(
+        widen_kernel,
+        out_shape=(
+            jax.ShapeDtypeStruct((rank, width), jnp.float32),
+            jax.ShapeDtypeStruct((rank, (columns - width) // 2), jnp.float32),
+        ),
+        in_specs=[whole],
+        out_specs=(whole, whole),
+        compiler_params=pltpu.CompilerParams(vmem_limit_bytes=8 * 1024 * 1024),
+        name="widen",
+    )(both)
+
+
 def exchange(blocks, axis, groups=None):
     return lax.all_to_all(blocks, axis, split_axis=0, concat_axis=0, tiled=True, axis_index_groups=groups)
 
@@ -96,7 +142,7 @@
     return jnp.sum(exchange(mine, "dp", y_groups()).astype(jnp.float32), axis=0)
 
 
-def pair_sum(part, masks):
+def with_pair(part, masks):
     replicas, experts = lax.axis_size("dp"), lax.axis_size("expert")
     pairs = []
     for replica in range(replicas):
@@ -105,13 +151,7 @@
             partner = (z ^ masks[expert % 2]) * Y_SIZE + y
             pairs.append((replica * experts + expert, partner * experts + expert))
     own = narrow(part)
-    other = lax.ppermute(own.astype(jnp.bfloat16), ("dp", "expert"), pairs)
-    return own + other.astype(jnp.float32)
-
-
-def gather_over_y(part):
-    copies = jnp.broadcast_to(part.astype(jnp.bfloat16)[None], (Y_SIZE,) + part.shape)
-    return exchange(copies, "dp", y_groups()).reshape(-1, part.shape[1])
+    return own, lax.ppermute(own.astype(jnp.bfloat16), ("dp", "expert"), pairs)
 
 
 def shards(grad_out, expert_ids, gate_weight, saved_hidden, down_weight, adapter_a, adapter_b):
@@ -139,8 +179,10 @@
     part_a = adapter_scale * (both[: factor_a.shape[0]] + both[factor_a.shape[0] :])
     over_y = sum_over_y(jnp.concatenate([part_b, part_a], axis=1))
     near, far = 1, lax.axis_size("dp") // Y_SIZE - 1
-    half_z = pair_sum(over_y, (near, far))
-    summed = gather_over_y(pair_sum(half_z, (far, near))).astype(jnp.float32)
+    own, other = with_pair(over_y, (near, far))
+    own, other = with_pair(own + other.astype(jnp.float32), (far, near))
+    summed = exchange(last_sum(own, other, Y_SIZE, width), "dp", y_groups())
+    grad_b, grad_a = widen(summed.reshape(factor_b.shape[0], -1), width)
 
     projected = lax.dot_general(rows, weight, over_columns, preferred_element_type=jnp.float32)
     back = jnp.dot(rounded_proj, factor_a, preferred_element_type=jnp.float32)
@@ -151,7 +193,7 @@
     came_back = exchange(gate_terms.reshape(experts, capacity), "expert").reshape(-1)
     chosen = jnp.arange(slots, dtype=jnp.int32)[:, None] == slot_index
     gate_grad = jnp.sum(jnp.where(chosen, came_back[:, None], 0.0), axis=0) / gates
-    return (hidden_gradient.reshape(saved_hidden.shape), gate_grad, summed[None, :, width:], summed[None, :, :width])
+    return (hidden_gradient.reshape(saved_hidden.shape), gate_grad, grad_a[None], grad_b[None])
 
 
 def solution(mesh):

time: 165 us -> 165 us (level)
  local copies, waits for them, and re-layouts: 4.42 us -> 2.2 us
    broadcast_in_dim x3 -> x0, local copies, waits for them, and re-layouts: 2.21 us -> none  [the longest x1 0.83 us: shards(): summed[None, :, :width]]
where the time goes in v5:
time: 165 us
  waiting for transfers between devices  88 us (53%)
  starting transfers between devices  58.4 us (35%)
  matrix products  7.43 us (5%)
  Pallas kernels  5.48 us (3%)
  local copies, waits for them, and re-layouts  2.2 us (1%)
  other arithmetic  2.19 us (1%)
    all_to_all x4, waiting for transfers between devices, exchange(): lax.all_to_all(blocks, axis, split_axis=0, concat_axis=0, tiled=True, axi...  76.4 us
    all_to_all x4, starting transfers between devices, exchange(): lax.all_to_all(blocks, axis, split_axis=0, concat_axis=0, tiled=True, axi...  39 us
    ppermute x2, starting transfers between devices, with_pair(): lax.ppermute(own.astype(jnp.bfloat16), ('dp', 'expert'), pairs)  19.4 us
    ppermute x2, waiting for transfers between devices, with_pair(): lax.ppermute(own.astype(jnp.bfloat16), ('dp', 'expert'), pairs)  11.6 us
    dot_general x1, matrix products, shards(): lax.dot_general(rows, weight, over_columns, preferred_element_type=jnp.fl...  5.1 us
    pallas_call x1, Pallas kernels, pack_rows(): pl.pallas_call(partial(pack_kernel, capacity), out_shape=(jax.ShapeDtypeS...  3.87 us
  transfers between devices with their start and end apart: 6, of which 4 were waited for; matrix products, arithmetic and copies ran while one was open for 5% of the time, Pallas kernels for 0%

profile of v5, /device:TPU:133, one launch (start us, length us, event | category | flops | bytes accessed | tf_op | source)
XLA Modules:
  0.0 164.5 jit_solution(15900049933884316603)
XLA Ops:
  0.6 0.0 copy-start
  0.6 3.9 %pack_rows.1 = (bf16[1536,512]{1,0:T(8,128)(2,1)}, s32[1,128]{1,0:T(1,128)}) custom-call(s32[1,128]{1,0:T(1,128)} %bitcast.42, bf16[1,128]{1,0:T(2,128)(2,1)} %bitcast.43, bf16[128,4096]{1,0:T(8,128)(2,1)} %grad_hbm.1), custom_call_target="tpu_custom_call" | custom-call | tf_op jit(solution)/shard_map/pack_rows/pallas_call | solution.py:60
  4.5 0.0 copy-start.1
  4.5 0.0 copy-start.3
  4.5 16.1 %all-to-all-start = ((bf16[64,24,512]{2,1,0:T(8,128)(2,1)}), bf16[64,24,512]{2,1,0:T(8,128)(2,1)S(1)}, u32[]{:S(2)}, u32[]{:S(2)}) async-start(bf16[64,24,512]{2,1,0:T(8,128)(2,1)} %bitcast.41), calls=%async_computation | async-start | bytes 3145728 | tf_op jit(solution)/shard_map/all_to_all | solution.py:127
  20.7 0.0 copy-done.1
  20.7 0.0 copy-done.3
  20.7 0.2 convolution_convert_fusion
  20.9 67.9 %all-to-all-done = bf16[64,24,512]{2,1,0:T(8,128)(2,1)S(1)} async-done(((bf16[64,24,512]{2,1,0:T(8,128)(2,1)}), bf16[64,24,512]{2,1,0:T(8,128)(2,1)S(1)}, u32[]{:S(2)}, u32[]{:S(2)}) %all-to-all-start) | async-done | bytes 1572896 | tf_op jit(solution)/shard_map/all_to_all | solution.py:127
  88.7 0.8 reshape.43
  89.5 0.0 copy-start.2
  89.5 0.4 fusion.3
  89.9 0.0 copy-done
  89.9 0.6 reduce-precision_convert_fusion.1
  90.6 0.0 copy-done.2
  90.6 0.2 fusion.7
  90.8 0.7 pad_maximum_fusion
  91.5 3.5 %all-to-all-start.1 = ((bf16[4,8,4864]{2,1,0:T(8,128)(2,1)}), bf16[4,8,4864]{2,1,0:T(8,128)(2,1)S(1)}, u32[]{:S(2)}, u32[]{:S(2)}) async-start(bf16[4,8,4864]{2,1,0:T(8,128)(2,1)} %pad_maximum_fusion), calls=%async_computation.1 | async-start | bytes 622592 | tf_op jit(solution)/shard_map/all_to_all | solution.py:127
  95.0 5.1 %multiply_reduce_fusion = (f32[192]{0:T(256)S(1)}, f32[192,768]{1,0:T(8,128)S(1)}) fusion(bf16[1,1,192,768]{3,2,1,0:T(8,128)(2,1)S(1)} %copy-done.2, bf16[192,4096]{1,0:T(8,128)(2,1)S(1)} %reshape.43, bf16[1,768,4096]{2,1,0:T(8,128)(2,1)} %param.11), kind=kOutput, calls=%fused_computation.11 | convolution fusion | flops 1208401664 | bytes 8749824 | tf_op jit(solution)/shard_map/dot_general | solution.py:187
  100.1 0.9 all-to-all-done.1
  101.1 0.0 copy-start.5
  101.1 0.0 copy-start.4
  101.1 14.0 %collective-permute-start = (bf16[8,4864]{1,0:T(8,128)(2,1)S(1)}, bf16[8,4864]{1,0:T(8,128)(2,1)S(1)}, u32[]{:S(2)}, u32[]{:S(2)}) collective-permute-start(bf16[8,4864]{1,0:T(8,128)(2,1)S(1)} %reduce-precision_convert_fusion), channel_id=1, source_target_pairs={{0,256},{1,769},{2,258},{3,771},{4,260},{5,773},{6,262},{7,775},{8... | collective-permute-start | bytes 233480 | tf_op jit(solution)/shard_map/ppermute | solution.py:154
  115.1 0.8 all_to_all.17
  115.9 16.0 %all-to-all-start.2 = ((f32[64,1,3]{2,1,0:T(1,128)}), f32[64,1,3]{2,1,0:T(1,128)S(1)}, u32[]{:S(2)}, u32[]{:S(2)}) async-start(f32[64,1,3]{2,1,0:T(1,128)} %bitcast.11), calls=%async_computation.2 | async-start | bytes 65536 | tf_op jit(solution)/shard_map/all_to_all | solution.py:127
  131.9 0.0 collective-permute-done
  131.9 5.4 %collective-permute-start.1 = (bf16[8,4864]{1,0:T(8,128)(2,1)S(1)}, bf16[8,4864]{1,0:T(8,128)(2,1)S(1)}, u32[]{:S(2)}, u32[]{:S(2)}) collective-permute-start(bf16[8,4864]{1,0:T(8,128)(2,1)S(1)} %get-tuple-element.14), channel_id=1, source_target_pairs={{0,768},{1,257},{2,770},{3,259},{4,772},{5,261},{6,774},{7,263},{8... | collective-permute-start | bytes 233480 | tf_op jit(solution)/shard_map/ppermute | solution.py:154
  137.3 1.0 fusion.6
  138.3 0.0 all-to-all-done.2
  138.3 0.5 broadcast.3
  138.8 0.7 reduce.3
  139.5 0.1 broadcast_in_dim.21
  139.7 11.6 %collective-permute-done.1.other_ref = bf16[8,4864]{1,0:T(8,128)(2,1)S(1)} collective-permute-done((bf16[8,4864]{1,0:T(8,128)(2,1)S(1)}, bf16[8,4864]{1,0:T(8,128)(2,1)S(1)}, u32[]{:S(2)}, u32[]{:S(2)}) %collective-permute-start.1) | collective-permute-done | bytes 77856 | tf_op jit(solution)/shard_map/ppermute | solution.py:154
  151.2 0.8 last_sum.1
  152.0 3.5 %all-to-all-start.3 = ((bf16[4,8,5632]{2,1,0:T(8,128)(2,1)}), bf16[4,8,5632]{2,1,0:T(8,128)(2,1)S(1)}, u32[]{:S(2)}, u32[]{:S(2)}) async-start(bf16[4,8,5632]{2,1,0:T(8,128)(2,1)} %last_sum.1), calls=%async_computation.3 | async-start | bytes 720896 | tf_op jit(solution)/shard_map/all_to_all | solution.py:127
  155.5 0.0 copy-done.5
  155.5 0.1 select_reduce_fusion
  155.6 0.0 copy-done.4
  155.6 0.5 convert_divide_fusion
  156.1 7.6 %all-to-all-done.3 = bf16[4,8,5632]{2,1,0:T(8,128)(2,1)S(1)} async-done(((bf16[4,8,5632]{2,1,0:T(8,128)(2,1)}), bf16[4,8,5632]{2,1,0:T(8,128)(2,1)S(1)}, u32[]{:S(2)}, u32[]{:S(2)}) %all-to-all-start.3) | async-done | bytes 360480 | tf_op jit(solution)/shard_map/all_to_all | solution.py:127
  163.7 0.8 widen.1
  (5 shorter events, 0.1 us)
Async XLA Ops:
  0.6 89.3 %copy-start = (bf16[1,32,4096]{2,1,0:T(8,128)(2,1)S(1)}, bf16[1,32,4096]{2,1,0:T(8,128)(2,1)}, u32[]{:S(2)}) copy-start(bf16[1,32,4096]{2,1,0:T(8,128)(2,1)} %param.13) | copy-start | bytes 786436
  4.5 16.2 %copy-start.1 = (bf16[1,1,192,768]{3,2,1,0:T(8,128)(2,1)S(1)}, bf16[1,1,192,768]{3,2,1,0:T(8,128)(2,1)}, u32[]{:S(2)}) copy-start(bf16[1,1,192,768]{3,2,1,0:T(8,128)(2,1)} %param.10) | copy-start | bytes 884740
  4.5 16.2 %copy-start.3 = (bf16[1,32,768]{2,1,0:T(8,128)(2,1)S(1)}, bf16[1,32,768]{2,1,0:T(8,128)(2,1)}, u32[]{:S(2)}) copy-start(bf16[1,32,768]{2,1,0:T(8,128)(2,1)} %param.12) | copy-start | bytes 147460
  4.5 84.2 %all-to-all-start = ((bf16[64,24,512]{2,1,0:T(8,128)(2,1)}), bf16[64,24,512]{2,1,0:T(8,128)(2,1)S(1)}, u32[]{:S(2)}, u32[]{:S(2)}) async-start(bf16[64,24,512]{2,1,0:T(8,128)(2,1)} %bitcast.41), calls=%async_computation | async-start | bytes 3145728 | tf_op jit(solution)/shard_map/all_to_all | solution.py:127
  89.5 1.0 copy-start.2
  91.5 9.5 %all-to-all-start.1 = ((bf16[4,8,4864]{2,1,0:T(8,128)(2,1)}), bf16[4,8,4864]{2,1,0:T(8,128)(2,1)S(1)}, u32[]{:S(2)}, u32[]{:S(2)}) async-start(bf16[4,8,4864]{2,1,0:T(8,128)(2,1)} %pad_maximum_fusion), calls=%async_computation.1 | async-start | bytes 622592 | tf_op jit(solution)/shard_map/all_to_all | solution.py:127
  101.1 54.4 %copy-start.5 = (s32[1,128]{1,0:T(1,128)S(1)}, s32[1,128]{1,0:T(1,128)}, u32[]{:S(2)}) copy-start(s32[1,128]{1,0:T(1,128)} %get-tuple-element.10) | copy-start | bytes 1540
  101.1 54.5 %copy-start.4 = (bf16[128]{0:T(256)(128)(2,1)S(1)}, bf16[128]{0:T(256)(128)(2,1)}, u32[]{:S(2)}) copy-start(bf16[128]{0:T(256)(128)(2,1)} %param.9) | copy-start | bytes 772
  101.1 30.8 %collective-permute-start = (bf16[8,4864]{1,0:T(8,128)(2,1)S(1)}, bf16[8,4864]{1,0:T(8,128)(2,1)S(1)}, u32[]{:S(2)}, u32[]{:S(2)}) collective-permute-start(bf16[8,4864]{1,0:T(8,128)(2,1)S(1)} %reduce-precision_convert_fusion), channel_id=1, source_target_pairs={{0,256},{1,769},{2,258},{3,771},{4,260},{5,773},{6,262},{7,775},{8... | collective-permute-start | bytes 233480 | tf_op jit(solution)/shard_map/ppermute | solution.py:154
  115.9 22.4 %all-to-all-start.2 = ((f32[64,1,3]{2,1,0:T(1,128)}), f32[64,1,3]{2,1,0:T(1,128)S(1)}, u32[]{:S(2)}, u32[]{:S(2)}) async-start(f32[64,1,3]{2,1,0:T(1,128)} %bitcast.11), calls=%async_computation.2 | async-start | bytes 65536 | tf_op jit(solution)/shard_map/all_to_all | solution.py:127
  131.9 19.3 %collective-permute-start.1 = (bf16[8,4864]{1,0:T(8,128)(2,1)S(1)}, bf16[8,4864]{1,0:T(8,128)(2,1)S(1)}, u32[]{:S(2)}, u32[]{:S(2)}) collective-permute-start(bf16[8,4864]{1,0:T(8,128)(2,1)S(1)} %get-tuple-element.14), channel_id=1, source_target_pairs={{0,768},{1,257},{2,770},{3,259},{4,772},{5,261},{6,774},{7,263},{8... | collective-permute-start | bytes 233480 | tf_op jit(solution)/shard_map/ppermute | solution.py:154
  152.0 11.7 %all-to-all-start.3 = ((bf16[4,8,5632]{2,1,0:T(8,128)(2,1)}), bf16[4,8,5632]{2,1,0:T(8,128)(2,1)S(1)}, u32[]{:S(2)}, u32[]{:S(2)}) async-start(bf16[4,8,5632]{2,1,0:T(8,128)(2,1)} %last_sum.1), calls=%async_computation.3 | async-start | bytes 720896 | tf_op jit(solution)/shard_map/all_to_all | solution.py:127

commit v6 on v5

--- a/solution.py
+++ b/solution.py
@@ -11,7 +11,7 @@
 Y_SIZE = 4
 SUBLANES = 8
 LANES = 128
-GRAD_PARTS = 4
+GRAD_PARTS = 8
 
 
 def pack_kernel(capacity, ids_hbm, gate_hbm, grad_hbm, packed_ref, slot_ref, ids_ref, gate_ref, grad_ref, spread, sems):
@@ -179,8 +179,8 @@
     part_a = adapter_scale * (both[: factor_a.shape[0]] + both[factor_a.shape[0] :])
     over_y = sum_over_y(jnp.concatenate([part_b, part_a], axis=1))
     near, far = 1, lax.axis_size("dp") // Y_SIZE - 1
-    own, other = with_pair(over_y, (near, far))
-    own, other = with_pair(own + other.astype(jnp.float32), (far, near))
+    own, other = with_pair(over_y, (far, near))
+    own, other = with_pair(own + other.astype(jnp.float32), (near, far))
     summed = exchange(last_sum(own, other, Y_SIZE, width), "dp", y_groups())
     grad_b, grad_a = widen(summed.reshape(factor_b.shape[0], -1), width)
 

time: 165 us -> 165 us (level)
  the two profiles are of different devices: /device:TPU:133 before, /device:TPU:132 now
where the time goes in v6:
time: 165 us
  waiting for transfers between devices  87.1 us (53%)
  starting transfers between devices  59.2 us (36%)
  matrix products  7.44 us (5%)
  Pallas kernels  5.97 us (4%)
  local copies, waits for them, and re-layouts  2.2 us (1%)
  other arithmetic  2.19 us (1%)
    all_to_all x4, waiting for transfers between devices, exchange(): lax.all_to_all(blocks, axis, split_axis=0, concat_axis=0, tiled=True, axi...  77 us
    all_to_all x4, starting transfers between devices, exchange(): lax.all_to_all(blocks, axis, split_axis=0, concat_axis=0, tiled=True, axi...  35.9 us
    ppermute x2, starting transfers between devices, with_pair(): lax.ppermute(own.astype(jnp.bfloat16), ('dp', 'expert'), pairs)  23.4 us
    ppermute x2, waiting for transfers between devices, with_pair(): lax.ppermute(own.astype(jnp.bfloat16), ('dp', 'expert'), pairs)  10 us
    dot_general x1, matrix products, shards(): lax.dot_general(rows, weight, over_columns, preferred_element_type=jnp.fl...  5.1 us
    pallas_call x1, Pallas kernels, pack_rows(): pl.pallas_call(partial(pack_kernel, capacity), out_shape=(jax.ShapeDtypeS...  4.36 us
  transfers between devices with their start and end apart: 6, of which 4 were waited for; matrix products, arithmetic and copies ran while one was open for 5% of the time, Pallas kernels for 0%

profile of v6, /device:TPU:132, one launch (start us, length us, event | category | flops | bytes accessed | tf_op | source)
XLA Modules:
  0.0 165.0 jit_solution(16211512246024385411)
XLA Ops:
  0.6 0.0 copy-start
  0.6 4.4 %pack_rows.1 = (bf16[1536,512]{1,0:T(8,128)(2,1)}, s32[1,128]{1,0:T(1,128)}) custom-call(s32[1,128]{1,0:T(1,128)} %bitcast.42, bf16[1,128]{1,0:T(2,128)(2,1)} %bitcast.43, bf16[128,4096]{1,0:T(8,128)(2,1)} %grad_hbm.1), custom_call_target="tpu_custom_call" | custom-call | tf_op jit(solution)/shard_map/pack_rows/pallas_call | solution.py:60
  5.0 0.0 copy-start.1
  5.0 0.0 copy-start.3
  5.0 15.8 %all-to-all-start = ((bf16[64,24,512]{2,1,0:T(8,128)(2,1)}), bf16[64,24,512]{2,1,0:T(8,128)(2,1)S(1)}, u32[]{:S(2)}, u32[]{:S(2)}) async-start(bf16[64,24,512]{2,1,0:T(8,128)(2,1)} %bitcast.41), calls=%async_computation | async-start | bytes 3145728 | tf_op jit(solution)/shard_map/all_to_all | solution.py:127
  20.9 0.0 copy-done.1
  20.9 0.0 copy-done.3
  20.9 0.2 convolution_convert_fusion
  21.1 68.4 %all-to-all-done = bf16[64,24,512]{2,1,0:T(8,128)(2,1)S(1)} async-done(((bf16[64,24,512]{2,1,0:T(8,128)(2,1)}), bf16[64,24,512]{2,1,0:T(8,128)(2,1)S(1)}, u32[]{:S(2)}, u32[]{:S(2)}) %all-to-all-start) | async-done | bytes 1572896 | tf_op jit(solution)/shard_map/all_to_all | solution.py:127
  89.4 0.8 reshape.43
  90.2 0.0 copy-start.2
  90.2 0.4 fusion.3
  90.6 0.0 copy-done
  90.6 0.6 reduce-precision_convert_fusion.1
  91.2 0.0 copy-done.2
  91.2 0.2 fusion.7
  91.5 0.7 pad_maximum_fusion
  92.2 3.5 %all-to-all-start.1 = ((bf16[4,8,4864]{2,1,0:T(8,128)(2,1)}), bf16[4,8,4864]{2,1,0:T(8,128)(2,1)S(1)}, u32[]{:S(2)}, u32[]{:S(2)}) async-start(bf16[4,8,4864]{2,1,0:T(8,128)(2,1)} %pad_maximum_fusion), calls=%async_computation.1 | async-start | bytes 622592 | tf_op jit(solution)/shard_map/all_to_all | solution.py:127
  95.7 5.1 %multiply_reduce_fusion = (f32[192]{0:T(256)S(1)}, f32[192,768]{1,0:T(8,128)S(1)}) fusion(bf16[1,1,192,768]{3,2,1,0:T(8,128)(2,1)S(1)} %copy-done.2, bf16[192,4096]{1,0:T(8,128)(2,1)S(1)} %reshape.43, bf16[1,768,4096]{2,1,0:T(8,128)(2,1)} %param.11), kind=kOutput, calls=%fused_computation.11 | convolution fusion | flops 1208401664 | bytes 8749824 | tf_op jit(solution)/shard_map/dot_general | solution.py:187
  100.8 2.1 %all-to-all-done.1 = bf16[4,8,4864]{2,1,0:T(8,128)(2,1)S(1)} async-done(((bf16[4,8,4864]{2,1,0:T(8,128)(2,1)}), bf16[4,8,4864]{2,1,0:T(8,128)(2,1)S(1)}, u32[]{:S(2)}, u32[]{:S(2)}) %all-to-all-start.1) | async-done | bytes 311328 | tf_op jit(solution)/shard_map/all_to_all | solution.py:127
  102.9 0.0 copy-start.5
  103.0 0.0 copy-start.4
  103.0 14.9 %collective-permute-start = (bf16[8,4864]{1,0:T(8,128)(2,1)S(1)}, bf16[8,4864]{1,0:T(8,128)(2,1)S(1)}, u32[]{:S(2)}, u32[]{:S(2)}) collective-permute-start(bf16[8,4864]{1,0:T(8,128)(2,1)S(1)} %reduce-precision_convert_fusion), channel_id=1, source_target_pairs={{0,768},{1,257},{2,770},{3,259},{4,772},{5,261},{6,774},{7,263},{8... | collective-permute-start | bytes 233480 | tf_op jit(solution)/shard_map/ppermute | solution.py:154
  117.9 0.8 all_to_all.17
  118.7 13.1 %all-to-all-start.2 = ((f32[64,1,3]{2,1,0:T(1,128)}), f32[64,1,3]{2,1,0:T(1,128)S(1)}, u32[]{:S(2)}, u32[]{:S(2)}) async-start(f32[64,1,3]{2,1,0:T(1,128)} %bitcast.11), calls=%async_computation.2 | async-start | bytes 65536 | tf_op jit(solution)/shard_map/all_to_all | solution.py:127
  131.8 0.0 collective-permute-done
  131.9 8.4 %collective-permute-start.1 = (bf16[8,4864]{1,0:T(8,128)(2,1)S(1)}, bf16[8,4864]{1,0:T(8,128)(2,1)S(1)}, u32[]{:S(2)}, u32[]{:S(2)}) collective-permute-start(bf16[8,4864]{1,0:T(8,128)(2,1)S(1)} %get-tuple-element.14), channel_id=1, source_target_pairs={{0,256},{1,769},{2,258},{3,771},{4,260},{5,773},{6,262},{7,775},{8... | collective-permute-start | bytes 233480 | tf_op jit(solution)/shard_map/ppermute | solution.py:154
  140.3 1.0 fusion.6
  141.3 0.0 all-to-all-done.2
  141.3 0.5 broadcast.3
  141.8 0.7 reduce.3
  142.6 0.1 broadcast_in_dim.21
  142.7 10.0 %collective-permute-done.1.other_ref = bf16[8,4864]{1,0:T(8,128)(2,1)S(1)} collective-permute-done((bf16[8,4864]{1,0:T(8,128)(2,1)S(1)}, bf16[8,4864]{1,0:T(8,128)(2,1)S(1)}, u32[]{:S(2)}, u32[]{:S(2)}) %collective-permute-start.1) | collective-permute-done | bytes 77856 | tf_op jit(solution)/shard_map/ppermute | solution.py:154
  152.7 0.8 last_sum.1
  153.5 3.5 %all-to-all-start.3 = ((bf16[4,8,5632]{2,1,0:T(8,128)(2,1)}), bf16[4,8,5632]{2,1,0:T(8,128)(2,1)S(1)}, u32[]{:S(2)}, u32[]{:S(2)}) async-start(bf16[4,8,5632]{2,1,0:T(8,128)(2,1)} %last_sum.1), calls=%async_computation.3 | async-start | bytes 720896 | tf_op jit(solution)/shard_map/all_to_all | solution.py:127
  156.9 0.0 copy-done.5
  157.0 0.1 select_reduce_fusion
  157.1 0.0 copy-done.4
  157.1 0.5 convert_divide_fusion
  157.6 6.5 %all-to-all-done.3 = bf16[4,8,5632]{2,1,0:T(8,128)(2,1)S(1)} async-done(((bf16[4,8,5632]{2,1,0:T(8,128)(2,1)}), bf16[4,8,5632]{2,1,0:T(8,128)(2,1)S(1)}, u32[]{:S(2)}, u32[]{:S(2)}) %all-to-all-start.3) | async-done | bytes 360480 | tf_op jit(solution)/shard_map/all_to_all | solution.py:127
  164.1 0.8 widen.1
  (5 shorter events, 0.1 us)
Async XLA Ops:
  0.6 90.0 %copy-start = (bf16[1,32,4096]{2,1,0:T(8,128)(2,1)S(1)}, bf16[1,32,4096]{2,1,0:T(8,128)(2,1)}, u32[]{:S(2)}) copy-start(bf16[1,32,4096]{2,1,0:T(8,128)(2,1)} %param.13) | copy-start | bytes 786436
  5.0 15.9 %copy-start.1 = (bf16[1,1,192,768]{3,2,1,0:T(8,128)(2,1)S(1)}, bf16[1,1,192,768]{3,2,1,0:T(8,128)(2,1)}, u32[]{:S(2)}) copy-start(bf16[1,1,192,768]{3,2,1,0:T(8,128)(2,1)} %param.10) | copy-start | bytes 884740
  5.0 15.9 %copy-start.3 = (bf16[1,32,768]{2,1,0:T(8,128)(2,1)S(1)}, bf16[1,32,768]{2,1,0:T(8,128)(2,1)}, u32[]{:S(2)}) copy-start(bf16[1,32,768]{2,1,0:T(8,128)(2,1)} %param.12) | copy-start | bytes 147460
  5.0 84.4 %all-to-all-start = ((bf16[64,24,512]{2,1,0:T(8,128)(2,1)}), bf16[64,24,512]{2,1,0:T(8,128)(2,1)S(1)}, u32[]{:S(2)}, u32[]{:S(2)}) async-start(bf16[64,24,512]{2,1,0:T(8,128)(2,1)} %bitcast.41), calls=%async_computation | async-start | bytes 3145728 | tf_op jit(solution)/shard_map/all_to_all | solution.py:127
  90.2 1.0 copy-start.2
  92.2 10.7 %all-to-all-start.1 = ((bf16[4,8,4864]{2,1,0:T(8,128)(2,1)}), bf16[4,8,4864]{2,1,0:T(8,128)(2,1)S(1)}, u32[]{:S(2)}, u32[]{:S(2)}) async-start(bf16[4,8,4864]{2,1,0:T(8,128)(2,1)} %pad_maximum_fusion), calls=%async_computation.1 | async-start | bytes 622592 | tf_op jit(solution)/shard_map/all_to_all | solution.py:127
  102.9 54.0 %copy-start.5 = (s32[1,128]{1,0:T(1,128)S(1)}, s32[1,128]{1,0:T(1,128)}, u32[]{:S(2)}) copy-start(s32[1,128]{1,0:T(1,128)} %get-tuple-element.10) | copy-start | bytes 1540
  103.0 54.1 %copy-start.4 = (bf16[128]{0:T(256)(128)(2,1)S(1)}, bf16[128]{0:T(256)(128)(2,1)}, u32[]{:S(2)}) copy-start(bf16[128]{0:T(256)(128)(2,1)} %param.9) | copy-start | bytes 772
  103.0 28.8 %collective-permute-start = (bf16[8,4864]{1,0:T(8,128)(2,1)S(1)}, bf16[8,4864]{1,0:T(8,128)(2,1)S(1)}, u32[]{:S(2)}, u32[]{:S(2)}) collective-permute-start(bf16[8,4864]{1,0:T(8,128)(2,1)S(1)} %reduce-precision_convert_fusion), channel_id=1, source_target_pairs={{0,768},{1,257},{2,770},{3,259},{4,772},{5,261},{6,774},{7,263},{8... | collective-permute-start | bytes 233480 | tf_op jit(solution)/shard_map/ppermute | solution.py:154
  118.7 22.6 %all-to-all-start.2 = ((f32[64,1,3]{2,1,0:T(1,128)}), f32[64,1,3]{2,1,0:T(1,128)S(1)}, u32[]{:S(2)}, u32[]{:S(2)}) async-start(f32[64,1,3]{2,1,0:T(1,128)} %bitcast.11), calls=%async_computation.2 | async-start | bytes 65536 | tf_op jit(solution)/shard_map/all_to_all | solution.py:127
  131.9 20.8 %collective-permute-start.1 = (bf16[8,4864]{1,0:T(8,128)(2,1)S(1)}, bf16[8,4864]{1,0:T(8,128)(2,1)S(1)}, u32[]{:S(2)}, u32[]{:S(2)}) collective-permute-start(bf16[8,4864]{1,0:T(8,128)(2,1)S(1)} %get-tuple-element.14), channel_id=1, source_target_pairs={{0,256},{1,769},{2,258},{3,771},{4,260},{5,773},{6,262},{7,775},{8... | collective-permute-start | bytes 233480 | tf_op jit(solution)/shard_map/ppermute | solution.py:154
  153.5 10.6 %all-to-all-start.3 = ((bf16[4,8,5632]{2,1,0:T(8,128)(2,1)}), bf16[4,8,5632]{2,1,0:T(8,128)(2,1)S(1)}, u32[]{:S(2)}, u32[]{:S(2)}) async-start(bf16[4,8,5632]{2,1,0:T(8,128)(2,1)} %last_sum.1), calls=%async_computation.3 | async-start | bytes 720896 | tf_op jit(solution)/shard_map/all_to_all | solution.py:127
